TPU v7x, 32 devices: a whole 2x2x4 slice. The times are simulated.
32 devices in a mesh: lon: 4 (over y, core), lat: 8 (over z, x).
Axes of the slice: x: 2, y: 2, z: 4, core: 2. Of those that a mesh axis runs over, the one named last changes fastest.
Arguments:
- fine_state: bfloat16 [512, 512, 128], P('lon', 'lat'), may hold values from -6 to 6
- coarse_state: bfloat16 [32, 32, 512], P('lon', 'lat'), may hold values from -6 to 6
- norm_gains: float32 [2, 128], replicated, may hold values from 0.25 to 1.75
- kernels: bfloat16 [2, 3, 3, 128, 128], replicated, may hold values from -0.1875 to 0.1875
- token_gain: float32 [512], replicated, may hold values from 0.25 to 1.75
- head_gains: float32 [2, 64], replicated, may hold values from 1.2 to 2.2
- query_weight: bfloat16 [512, 512], replicated, may hold values from -0.25 to 0.25
- keyvalue_weight: bfloat16 [512, 1024], replicated, may hold values from -0.25 to 0.25
- output_weight: bfloat16 [512, 512], replicated, may hold values from -0.25 to 0.25
- expand_weight: bfloat16 [512, 128], replicated, may hold values from -0.25 to 0.25
Outputs:
- fine_result: bfloat16 [512, 512, 128], P('lon', 'lat')
- coarse_result: bfloat16 [32, 32, 512], P('lon', 'lat')
All inputs are finite; a program needn't handle non-finite values.
Results may differ from a plain program's by a relative error of at most 0.005.
Values may be sent and summed in bfloat16 or wider, within the bound.
A program may use at most 192 MiB of HBM per device.

v0:
```python
import math

import jax
import jax.numpy as jnp
from jax import lax
from jax.sharding import PartitionSpec as P


def padded_2(block, sides, width, periodic):
    for axis, dim in sides:
        count = lax.axis_size(axis)
        forward = [(i, i + 1) for i in range(count - 1)]
        if periodic:
            forward.append((count - 1, 0))
        backward = [(target, source) for source, target in forward]
        low = lax.ppermute(
            lax.slice_in_dim(block, block.shape[dim] - width, None, axis=dim), axis, forward
        )
        high = lax.ppermute(lax.slice_in_dim(block, 0, width, axis=dim), axis, backward)
        block = jnp.concatenate([low, block, high], axis=dim)
    return block


def rescale_rows(matrix, gain_row):
    return matrix * lax.rsqrt(jnp.mean(matrix * matrix, axis=-1, keepdims=True) + 1e-06) * gain_row


def rescale_heads(projected, gain_row):
    shaped = projected.reshape(projected.shape[0], -1, gain_row.shape[0])
    return rescale_rows(shaped, gain_row)


def convolve(padded, kernel):
    return lax.conv_general_dilated(
        padded[None],
        kernel,
        (1, 1),
        "VALID",
        dimension_numbers=("NHWC", "HWIO", "NHWC"),
        preferred_element_type=jnp.float32,
    )[0]


def attach_rims(hidden, rim_width):
    wrapped = padded_2(hidden, (("lon", 0),), rim_width, True)
    return padded_2(wrapped, (("lat", 1),), rim_width, False)


def local(
    fine_state,
    coarse_state,
    norm_gains,
    kernels,
    token_gain,
    head_gains,
    query_weight,
    keyvalue_weight,
    output_weight,
    expand_weight,
):
    width_all = query_weight.shape[0]
    head_size = head_gains.shape[1]
    head_count = width_all // head_size
    lon_tokens = coarse_state.shape[0]
    lat_tokens = coarse_state.shape[1]
    lon_cells, lat_cells, channels = fine_state.shape
    first_hidden = jax.nn.silu(rescale_rows(fine_state.astype(jnp.float32), norm_gains[0])).astype(
        jnp.bfloat16
    )
    first_output = convolve(attach_rims(first_hidden, 1), kernels[0])
    second_hidden = jax.nn.silu(rescale_rows(first_output, norm_gains[1])).astype(jnp.bfloat16)
    second_output = convolve(attach_rims(second_hidden, 1), kernels[1])
    tokens = coarse_state.reshape(-1, width_all)
    normed = rescale_rows(tokens.astype(jnp.float32), token_gain).astype(jnp.bfloat16)
    scale_factor = 1.0 / math.sqrt(head_size)
    queries = (
        rescale_heads(
            jnp.dot(normed, query_weight, preferred_element_type=jnp.float32), head_gains[0]
        )
        * scale_factor
    ).astype(jnp.bfloat16)
    projected = jnp.dot(normed, keyvalue_weight, preferred_element_type=jnp.float32)
    key_rows = (
        rescale_heads(projected[:, :width_all], head_gains[1])
        .astype(jnp.bfloat16)
        .reshape(-1, width_all)
    )
    value_rows = projected[:, width_all:].astype(jnp.bfloat16)
    key_rows, value_rows = (key_rows, value_rows)
    accumulate_key_rows = lax.all_gather(key_rows, ("lon", "lat"), axis=0, tiled=True)
    accumulate_value_rows = lax.all_gather(value_rows, ("lon", "lat"), axis=0, tiled=True)
    key_heads = accumulate_key_rows.reshape(accumulate_key_rows.shape[0], head_count, head_size)
    value_heads = accumulate_value_rows.reshape(
        accumulate_value_rows.shape[0], head_count, head_size
    )
    scores = jnp.einsum("thd,shd->hts", queries, key_heads, preferred_element_type=jnp.float32)
    weights = jnp.exp(scores)
    totals = jnp.sum(weights, axis=-1)
    summed = jnp.einsum(
        "hts,shd->thd",
        weights.astype(jnp.bfloat16),
        value_heads,
        preferred_element_type=jnp.float32,
    )
    summed, totals = (summed, totals)
    attended = (
        (summed / jnp.transpose(totals)[:, :, None]).reshape(-1, width_all).astype(jnp.bfloat16)
    )
    coarse_result = (
        tokens.astype(jnp.float32)
        + jnp.dot(attended, output_weight, preferred_element_type=jnp.float32)
    ).astype(jnp.bfloat16)
    lifted = jnp.dot(coarse_result, expand_weight, preferred_element_type=jnp.float32).reshape(
        lon_tokens, 1, lat_tokens, 1, channels
    )
    merged = (fine_state.astype(jnp.float32) + second_output).reshape(
        lon_tokens, lon_cells // lon_tokens, lat_tokens, lat_cells // lat_tokens, channels
    ) + lifted
    fine_result = merged.reshape(lon_cells, lat_cells, channels).astype(jnp.bfloat16)
    return (fine_result, coarse_result.reshape(lon_tokens, lat_tokens, width_all))


def solution(mesh):
    return jax.shard_map(
        local,
        mesh=mesh,
        in_specs=(
            P("lon", "lat", None),
            P("lon", "lat", None),
            P(),
            P(),
            P(),
            P(),
            P(),
            P(),
            P(),
            P(),
        ),
        out_specs=(P("lon", "lat", None), P("lon", "lat", None)),
        check_vma=False,
    )
```

profile of v0, /device:TPU:0, one launch (start us, length us, event | category | flops | bytes accessed | tf_op | source)
XLA Modules:
  0.0 145.7 jit_solution(11972331446261645339)
XLA Ops:
  7.2 0.9 multiply_reduce_fusion.2
  8.2 0.8 reshape.112
  8.9 0.8 slice_bitcast_fusion.3
  9.7 0.1 mul.176
  9.8 0.1 rsqrt.47
  9.9 1.0 fusion.43
  10.9 0.1 mul.170
  11.0 0.1 reduce_sum.58
  11.1 0.1 copy.53
  11.2 0.1 copy.54
  11.2 0.1 mul.171
  11.3 0.1 mul.172
  11.4 0.6 multiply_convert_fusion.3
  12.1 0.0 all-gather.3.cloned.1.call-start
  12.1 0.8 slice_bitcast_fusion.4
  12.9 3.4 %fusion.2 = f32[128,64]{0,1:T(8,128)S(1)} fusion(bf16[128,64,128]{2,1,0:T(8,128)(2,1)} %param.10), kind=kLoop, calls=%fused_computation.6 | loop fusion | flops 3137536 | bytes 2129920 | tf_op jit(solution)/shard_map/reduce_sum | solution.py:25
  16.3 3.4 %fusion.9 = bf16[128,64,128]{2,0,1:T(8,128)(2,1)S(1)} fusion(f32[128]{0:T(128)S(1)} %get-tuple-element.17, f32[128,64]{0,1:T(8,128)S(1)} %add_rsqrt_fusion.1, bf16[128,64,128]{2,1,0:T(8,128)(2,1)} %param.10), kind=kLoop, calls=%fused_computation.13 | loop fusion | flops 8388608 | bytes 4227584 | tf_op jit(solution)/shard_map/convert_element_type | solution.py:67
  19.8 0.1 fusion.54
  19.8 0.5 collective-permute-start
  20.3 2.0 %collective-permute-start.1 = (bf16[1,64,128]{2,0,1:T(2,128)(2,1)S(1)}, bf16[1,64,128]{2,0,1:T(2,128)(2,1)S(1)}, u32[]{:S(2)}, u32[]{:S(2)}) collective-permute-start(bf16[1,64,128]{2,0,1:T(2,128)(2,1)S(1)} %get-tuple-element.15), channel_id=1, source_target_pairs={{8,0},{16,8},{24,16},{0,24},{9,1},{17,9},{25,17},{1,25},{10,2},{18... | collective-permute-start | bytes 49160 | tf_op jit(solution)/shard_map/ppermute | solution.py:19
  22.3 0.6 slice.102
  23.0 0.9 collective-permute-done
  23.9 0.2 collective-permute-done.1
  24.1 4.0 %collective-permute-start.2 = (bf16[130,1,128]{2,0,1:T(8,128)(2,1)S(1)}, bf16[130,1,128]{2,0,1:T(8,128)(2,1)S(1)}, u32[]{:S(2)}, u32[]{:S(2)}) collective-permute-start(bf16[130,1,128]{2,0,1:T(8,128)(2,1)S(1)} %get-tuple-element.10), channel_id=1, source_target_pairs={{0,1},{1,2},{2,3},{3,4},{4,5},{5,6},{6,7},{8,9},{9,10},{10,11},{11... | collective-permute-start | bytes 99848 | tf_op jit(solution)/shard_map/ppermute | solution.py:16
  28.1 1.5 %collective-permute-start.3 = (bf16[130,1,128]{2,0,1:T(8,128)(2,1)S(1)}, bf16[130,1,128]{2,0,1:T(8,128)(2,1)S(1)}, u32[]{:S(2)}, u32[]{:S(2)}) collective-permute-start(bf16[130,1,128]{2,0,1:T(8,128)(2,1)S(1)} %get-tuple-element.11), channel_id=1, source_target_pairs={{1,0},{2,1},{3,2},{4,3},{5,4},{6,5},{7,6},{9,8},{10,9},{11,10},{12... | collective-permute-start | bytes 99848 | tf_op jit(solution)/shard_map/ppermute | solution.py:19
  29.6 0.1 multiply_convert_fusion.4
  29.7 2.0 %copy.52 = bf16[512,512]{0,1:T(8,128)(2,1)} copy(bf16[512,512]{1,0:T(8,128)(2,1)} %param.16) | data formatting | bytes 1048576 | tf_op args[6]
  31.8 2.2 %collective-permute-done.3 = bf16[130,1,128]{2,0,1:T(8,128)(2,1)S(1)} collective-permute-done((bf16[130,1,128]{2,0,1:T(8,128)(2,1)S(1)}, bf16[130,1,128]{2,0,1:T(8,128)(2,1)S(1)}, u32[]{:S(2)}, u32[]{:S(2)}) %collective-permute-start.3) | collective-permute-done | bytes 33312 | tf_op jit(solution)/shard_map/ppermute | solution.py:19
  33.9 1.7 %maximum_bitcast_fusion = bf16[130,1,66,128]{3,0,2,1:T(8,128)(2,1)S(1)} fusion(bf16[130,1,128]{2,0,1:T(8,128)(2,1)S(1)} %collective-permute-done.3, bf16[1,64,128]{2,0,1:T(2,128)(2,1)S(1)} %collective-permute-done.1, bf16[128,64,128]{2,0,1:T(8,128)(2,1)S(1)} %fusion.9, bf16[1,64,128]{2,0,1:T(2,128)(2,1)S(1)} %collective-permute-done, ...), kind=kLoop, calls=%fused_computation.34 | loop fusion | flops 10982400 | bytes 4392960 | tf_op jit(solution)/shard_map/broadcast_in_dim | solution.py:35
  35.7 0.2 pad
  35.9 0.3 copy.46
  36.2 0.1 slice.71
  36.4 0.4 copy-done.6
  36.7 5.7 %broadcast_select_fusion.1 = f32[128,8,9,128]{3,1,2,0:T(8,128)S(1)} fusion(pred[8,9]{0,1:T(8,128)(4,1)S(1)} %copy-done.7, bf16[130,1,7,2,128]{4,2,3,0,1:T(8,128)(2,1)S(1)} %slice.71, bf16[130,1,8,9,128]{4,2,3,0,1:T(8,128)(2,1)S(1)} %copy.46, bf16[2,3,3,128,128]{4,3,2,1,0:T(8,128)(2,1)S(1)} %copy-done.6), kind=kOutput, calls=%fused_computation.33 | convolution fusion | flops 2727874560 | bytes 7944192 | tf_op jit(solution)/shard_map/conv_general_dilated | solution.py:34
  42.4 0.9 copy.47
  43.3 1.2 multiply_reduce_fusion
  44.5 1.5 %multiply_convert_fusion = bf16[128,64,128]{2,0,1:T(8,128)(2,1)S(1)} fusion(f32[128,1,72,128]{3,0,2,1:T(8,128)S(1)} %bitcast.67, f32[128]{0:T(128)S(1)} %get-tuple-element.16, f32[128,64]{0,1:T(8,128)S(1)} %add_rsqrt_fusion), kind=kLoop, calls=%fused_computation.18 | loop fusion | flops 7340032 | bytes 6324736 | tf_op jit(solution)/shard_map/convert_element_type | solution.py:71
  46.0 0.1 fusion.53
  46.1 1.1 collective-permute-start.4
  47.2 0.7 collective-permute-start.5
  47.9 0.4 multiply_reduce_fusion.1
  48.3 1.1 collective-permute-done.4
  49.5 4.4 %collective-permute-start.6 = (bf16[130,1,128]{2,0,1:T(8,128)(2,1)S(1)}, bf16[130,1,128]{2,0,1:T(8,128)(2,1)S(1)}, u32[]{:S(2)}, u32[]{:S(2)}) collective-permute-start(bf16[130,1,128]{2,0,1:T(8,128)(2,1)S(1)} %get-tuple-element.8), channel_id=1, source_target_pairs={{0,1},{1,2},{2,3},{3,4},{4,5},{5,6},{6,7},{8,9},{9,10},{10,11},{11... | collective-permute-start | bytes 99848 | tf_op jit(solution)/shard_map/ppermute | solution.py:16
  53.9 1.5 %collective-permute-start.7 = (bf16[130,1,128]{2,0,1:T(8,128)(2,1)S(1)}, bf16[130,1,128]{2,0,1:T(8,128)(2,1)S(1)}, u32[]{:S(2)}, u32[]{:S(2)}) collective-permute-start(bf16[130,1,128]{2,0,1:T(8,128)(2,1)S(1)} %get-tuple-element.9), channel_id=1, source_target_pairs={{1,0},{2,1},{3,2},{4,3},{5,4},{6,5},{7,6},{9,8},{10,9},{11,10},{12... | collective-permute-start | bytes 99848 | tf_op jit(solution)/shard_map/ppermute | solution.py:19
  55.5 0.2 collective-permute-done.6
  55.7 4.0 %collective-permute-done.7 = bf16[130,1,128]{2,0,1:T(8,128)(2,1)S(1)} collective-permute-done((bf16[130,1,128]{2,0,1:T(8,128)(2,1)S(1)}, bf16[130,1,128]{2,0,1:T(8,128)(2,1)S(1)}, u32[]{:S(2)}, u32[]{:S(2)}) %collective-permute-start.7) | collective-permute-done | bytes 33312 | tf_op jit(solution)/shard_map/ppermute | solution.py:19
  59.8 1.8 %maximum_bitcast_fusion.1 = bf16[130,1,66,128]{3,0,2,1:T(8,128)(2,1)S(1)} fusion(bf16[130,1,128]{2,0,1:T(8,128)(2,1)S(1)} %collective-permute-done.7, bf16[1,64,128]{2,0,1:T(2,128)(2,1)S(1)} %collective-permute-done.5, bf16[128,64,128]{2,0,1:T(8,128)(2,1)S(1)} %multiply_convert_fusion, bf16[1,64,128]{2,0,1:T(2,128)(2,1)S(1)} %collective-permute-done.4, ...), kind=kLoop, calls=%fused_computation.35 | loop fusion | flops 10982400 | bytes 4392960 | tf_op jit(solution)/shard_map/broadcast_in_dim | solution.py:35
  61.5 0.2 pad.2
  61.7 0.3 copy.49
  62.0 0.1 slice.75
  62.2 5.9 %broadcast_select_fusion = f32[128,8,9,128]{3,1,2,0:T(8,128)S(1)} fusion(pred[8,9]{0,1:T(8,128)(4,1)S(1)} %copy-done.7, bf16[130,1,7,2,128]{4,2,3,0,1:T(8,128)(2,1)S(1)} %slice.75, bf16[130,1,8,9,128]{4,2,3,0,1:T(8,128)(2,1)S(1)} %copy.49, bf16[2,3,3,128,128]{4,3,2,1,0:T(8,128)(2,1)S(1)} %copy-done.6), kind=kOutput, calls=%fused_computation.32 | convolution fusion | flops 2727874560 | bytes 7944192 | tf_op jit(solution)/shard_map/conv_general_dilated | solution.py:34
  68.1 3.0 %copy.50 = f32[128,8,9,128]{3,0,2,1:T(8,128)} copy(f32[128,8,9,128]{3,1,2,0:T(8,128)S(1)} %broadcast_select_fusion) | data formatting | bytes 9437184 | tf_op jit(solution)/shard_map/conv_general_dilated | solution.py:34
  71.1 1.5 %copy.55 = bf16[1024,512]{0,1:T(8,128)(2,1)S(1)} copy(bf16[1024,512]{1,0:T(8,128)(2,1)} %all-gather.5.cloned.1.call-done) | data formatting | bytes 2097152 | tf_op jit(solution)/shard_map/all_gather | solution.py:90
  72.6 1.2 fusion.55
  73.8 51.6 %all-gather.3.cloned.1.call-done = bf16[1024,512]{1,0:T(8,128)(2,1)} async-done(((bf16[32,512]{1,0:T(8,128)(2,1)}), bf16[1024,512]{1,0:T(8,128)(2,1)}) %all-gather.3.cloned.1.call-update) | async-done | bytes 1048592 | tf_op jit(solution)/shard_map/all_gather | solution.py:91
  125.4 2.3 %copy.51 = bf16[1024,512]{0,1:T(8,128)(2,1)} copy(bf16[1024,512]{1,0:T(8,128)(2,1)} %all-gather.3.cloned.1.call-done) | data formatting | bytes 2097152 | tf_op jit(solution)/shard_map/all_gather | solution.py:91
  127.7 1.9 %fusion.33 = bf16[32,8,64]{2,0,1:T(8,128)(2,1)S(1)} fusion(bf16[1024,8,64]{0,2,1:T(8,128)(2,1)} %bitcast.74, bf16[8,32,1024]{2,1,0:T(8,128)(2,1)} %get-tuple-element.23, f32[32,8]{0,1:T(8,128)S(1)} %bitcast.76), kind=kOutput, calls=%fused_computation.41 | convolution fusion | flops 33587200 | bytes 1606656 | tf_op jit(solution)/shard_map/hts,shd->thd/dot_general | solution.py:99
  129.6 0.1 convert_element_type.65
  129.7 1.2 fusion.34
  131.0 0.6 reshape.97
  131.6 0.1 fusion.56
  131.8 0.5 add.82
  132.3 3.9 %fusion.11 = bf16[128,64,128]{2,0,1:T(8,128)(2,1)S(1)} fusion(f32[128,64,128]{2,0,1:T(8,128)S(1)} %bitcast.69, f32[128,1,72,128]{3,0,2,1:T(8,128)} %bitcast.68, bf16[128,64,128]{2,1,0:T(8,128)(2,1)S(1)} %copy-done.1), kind=kLoop, calls=%fused_computation.15 | loop fusion | flops 4194304 | bytes 12582912 | tf_op jit(solution)/shard_map/convert_element_type | solution.py:119
  136.2 2.7 %copy.58 = bf16[128,64,128]{2,1,0:T(8,128)(2,1)} copy(bf16[128,64,128]{2,0,1:T(8,128)(2,1)S(1)} %fusion.11) | data formatting | bytes 4194304
  (33 shorter events, 0.3 us)
Async XLA Ops:
  7.2 2.7 %copy-start = (bf16[512,1024]{1,0:T(8,128)(2,1)S(1)}, bf16[512,1024]{1,0:T(8,128)(2,1)}, u32[]{:S(2)}) copy-start(bf16[512,1024]{1,0:T(8,128)(2,1)} %param.17) | copy-start | bytes 3145732
  7.2 63.9 %all-gather.5.cloned.1.call-start = ((), (), s32[]{:S(2)}) async-start(), calls=%async_computation.1 | async-start | bytes 1081344 | tf_op jit(solution)/shard_map/all_gather | solution.py:90
  12.1 113.3 %all-gather.3.cloned.1.call-start = ((), (), s32[]{:S(2)}) async-start(), calls=%async_computation | async-start | bytes 1081344 | tf_op jit(solution)/shard_map/all_gather | solution.py:91
  12.9 16.7 %copy-start.3 = (bf16[8,4,512]{2,1,0:T(4,128)(2,1)S(1)}, bf16[8,4,512]{2,1,0:T(4,128)(2,1)}, u32[]{:S(2)}) copy-start(bf16[8,4,512]{2,1,0:T(4,128)(2,1)} %param.11) | copy-start | bytes 98308
  12.9 16.7 %copy-start.5 = (f32[512]{0:T(512)S(1)}, f32[512]{0:T(512)}, u32[]{:S(2)}) copy-start(f32[512]{0:T(512)} %param.14) | copy-start | bytes 6148
  19.8 4.1 %collective-permute-start = (bf16[1,64,128]{2,0,1:T(2,128)(2,1)S(1)}, bf16[1,64,128]{2,0,1:T(2,128)(2,1)S(1)}, u32[]{:S(2)}, u32[]{:S(2)}) collective-permute-start(bf16[1,64,128]{2,0,1:T(2,128)(2,1)S(1)} %get-tuple-element.14), channel_id=1, source_target_pairs={{0,8},{8,16},{16,24},{24,0},{1,9},{9,17},{17,25},{25,1},{2,10},{10... | collective-permute-start | bytes 49160 | tf_op jit(solution)/shard_map/ppermute | solution.py:16
  20.3 3.8 %collective-permute-start.1 = (bf16[1,64,128]{2,0,1:T(2,128)(2,1)S(1)}, bf16[1,64,128]{2,0,1:T(2,128)(2,1)S(1)}, u32[]{:S(2)}, u32[]{:S(2)}) collective-permute-start(bf16[1,64,128]{2,0,1:T(2,128)(2,1)S(1)} %get-tuple-element.15), channel_id=1, source_target_pairs={{8,0},{16,8},{24,16},{0,24},{9,1},{17,9},{25,17},{1,25},{10,2},{18... | collective-permute-start | bytes 49160 | tf_op jit(solution)/shard_map/ppermute | solution.py:19
  24.1 7.7 %collective-permute-start.2 = (bf16[130,1,128]{2,0,1:T(8,128)(2,1)S(1)}, bf16[130,1,128]{2,0,1:T(8,128)(2,1)S(1)}, u32[]{:S(2)}, u32[]{:S(2)}) collective-permute-start(bf16[130,1,128]{2,0,1:T(8,128)(2,1)S(1)} %get-tuple-element.10), channel_id=1, source_target_pairs={{0,1},{1,2},{2,3},{3,4},{4,5},{5,6},{6,7},{8,9},{9,10},{10,11},{11... | collective-permute-start | bytes 99848 | tf_op jit(solution)/shard_map/ppermute | solution.py:16
  28.1 5.8 %collective-permute-start.3 = (bf16[130,1,128]{2,0,1:T(8,128)(2,1)S(1)}, bf16[130,1,128]{2,0,1:T(8,128)(2,1)S(1)}, u32[]{:S(2)}, u32[]{:S(2)}) collective-permute-start(bf16[130,1,128]{2,0,1:T(8,128)(2,1)S(1)} %get-tuple-element.11), channel_id=1, source_target_pairs={{1,0},{2,1},{3,2},{4,3},{5,4},{6,5},{7,6},{9,8},{10,9},{11,10},{12... | collective-permute-start | bytes 99848 | tf_op jit(solution)/shard_map/ppermute | solution.py:19
  35.7 1.1 copy-start.6
  35.7 1.1 copy-start.7
  44.5 3.4 %copy-start.2 = (bf16[512,512]{0,1:T(8,128)(2,1)S(1)}, bf16[512,512]{0,1:T(8,128)(2,1)}, u32[]{:S(2)}) copy-start(bf16[512,512]{0,1:T(8,128)(2,1)} %copy.52) | copy-start | bytes 1572868
  46.1 3.4 %collective-permute-start.4 = (bf16[1,64,128]{2,0,1:T(2,128)(2,1)S(1)}, bf16[1,64,128]{2,0,1:T(2,128)(2,1)S(1)}, u32[]{:S(2)}, u32[]{:S(2)}) collective-permute-start(bf16[1,64,128]{2,0,1:T(2,128)(2,1)S(1)} %get-tuple-element.12), channel_id=1, source_target_pairs={{0,8},{8,16},{16,24},{24,0},{1,9},{9,17},{17,25},{25,1},{2,10},{10... | collective-permute-start | bytes 49160 | tf_op jit(solution)/shard_map/ppermute | solution.py:16
  47.2 2.3 %collective-permute-start.5 = (bf16[1,64,128]{2,0,1:T(2,128)(2,1)S(1)}, bf16[1,64,128]{2,0,1:T(2,128)(2,1)S(1)}, u32[]{:S(2)}, u32[]{:S(2)}) collective-permute-start(bf16[1,64,128]{2,0,1:T(2,128)(2,1)S(1)} %get-tuple-element.13), channel_id=1, source_target_pairs={{8,0},{16,8},{24,16},{0,24},{9,1},{17,9},{25,17},{1,25},{10,2},{18... | collective-permute-start | bytes 49160 | tf_op jit(solution)/shard_map/ppermute | solution.py:19
  49.5 6.2 %collective-permute-start.6 = (bf16[130,1,128]{2,0,1:T(8,128)(2,1)S(1)}, bf16[130,1,128]{2,0,1:T(8,128)(2,1)S(1)}, u32[]{:S(2)}, u32[]{:S(2)}) collective-permute-start(bf16[130,1,128]{2,0,1:T(8,128)(2,1)S(1)} %get-tuple-element.8), channel_id=1, source_target_pairs={{0,1},{1,2},{2,3},{3,4},{4,5},{5,6},{6,7},{8,9},{9,10},{10,11},{11... | collective-permute-start | bytes 99848 | tf_op jit(solution)/shard_map/ppermute | solution.py:16
  53.9 5.8 %collective-permute-start.7 = (bf16[130,1,128]{2,0,1:T(8,128)(2,1)S(1)}, bf16[130,1,128]{2,0,1:T(8,128)(2,1)S(1)}, u32[]{:S(2)}, u32[]{:S(2)}) collective-permute-start(bf16[130,1,128]{2,0,1:T(8,128)(2,1)S(1)} %get-tuple-element.9), channel_id=1, source_target_pairs={{1,0},{2,1},{3,2},{4,3},{5,4},{6,5},{7,6},{9,8},{10,9},{11,10},{12... | collective-permute-start | bytes 99848 | tf_op jit(solution)/shard_map/ppermute | solution.py:19
  71.1 60.5 %copy-start.4 = (bf16[512,128]{1,0:T(8,128)(2,1)S(1)}, bf16[512,128]{1,0:T(8,128)(2,1)}, u32[]{:S(2)}) copy-start(bf16[512,128]{1,0:T(8,128)(2,1)} %param.19) | copy-start | bytes 393220
  127.7 4.6 %copy-start.1 = (bf16[128,64,128]{2,1,0:T(8,128)(2,1)S(1)}, bf16[128,64,128]{2,1,0:T(8,128)(2,1)}, u32[]{:S(2)}) copy-start(bf16[128,64,128]{2,1,0:T(8,128)(2,1)} %param.10) | copy-start | bytes 6291460
Sparse Core Ops, SparseCore 0:
  12.2 57.2 all-gather.4
  73.0 52.3 all-gather.2
where the time goes:
time: 146 us
  waiting for transfers between devices  60.4 us (41%)
  local copies, waits for them, and re-layouts  19 us (13%)
  other arithmetic  18.7 us (13%)
  matrix products  17.5 us (12%)
  starting transfers between devices  15.8 us (11%)
  between operations  14.4 us (10%)
    all_gather x1, waiting for transfers between devices, local(): lax.all_gather(value_rows, ('lon', 'lat'), axis=0, tiled=True)  51.6 us
    conv_general_dilated x2, matrix products, convolve(): lax.conv_general_dilated(padded[None], kernel, (1, 1), 'VALID', dimension...  11.6 us
    ppermute x4, starting transfers between devices, padded_2(): lax.ppermute(lax.slice_in_dim(block, block.shape[dim] - width, None, axis...  9.99 us
    ppermute x4, waiting for transfers between devices, padded_2(): lax.ppermute(lax.slice_in_dim(block, 0, width, axis=dim), axis, backward)  6.44 us
    ppermute x4, starting transfers between devices, padded_2(): lax.ppermute(lax.slice_in_dim(block, 0, width, axis=dim), axis, backward)  5.7 us
    reduce_sum x4, other arithmetic, rescale_rows(): jnp.mean(matrix * matrix, axis=-1, keepdims=True) + 1e-06  5.57 us
    unnamed x18, local copies, waits for them, and re-layouts  5.14 us
    conv_general_dilated x6, local copies, waits for them, and re-layouts, convolve(): lax.conv_general_dilated(padded[None], kernel, (1, 1), 'VALID', dimension...  4.8 us
  transfers between devices with their start and end apart: 10, of which 7 were waited for; matrix products, arithmetic and copies ran while one was open for 25% of the time, Pallas kernels for 0%

commit v1 on v0

--- a/solution.py
+++ b/solution.py
@@ -79,16 +79,17 @@
         )
         * scale_factor
     ).astype(jnp.bfloat16)
-    projected = jnp.dot(normed, keyvalue_weight, preferred_element_type=jnp.float32)
+    all_tokens = lax.all_gather(tokens, ("lon", "lat"), axis=0, tiled=True)
+    all_normed = rescale_rows(all_tokens.astype(jnp.float32), token_gain).astype(jnp.bfloat16)
+    projected = jnp.dot(all_normed, keyvalue_weight, preferred_element_type=jnp.float32)
     key_rows = (
         rescale_heads(projected[:, :width_all], head_gains[1])
         .astype(jnp.bfloat16)
         .reshape(-1, width_all)
     )
     value_rows = projected[:, width_all:].astype(jnp.bfloat16)
-    key_rows, value_rows = (key_rows, value_rows)
-    accumulate_key_rows = lax.all_gather(key_rows, ("lon", "lat"), axis=0, tiled=True)
-    accumulate_value_rows = lax.all_gather(value_rows, ("lon", "lat"), axis=0, tiled=True)
+    accumulate_key_rows = key_rows
+    accumulate_value_rows = value_rows
     key_heads = accumulate_key_rows.reshape(accumulate_key_rows.shape[0], head_count, head_size)
     value_heads = accumulate_value_rows.reshape(
         accumulate_value_rows.shape[0], head_count, head_size

time: 146 us -> 96.5 us (0.66)
  waiting for transfers between devices: 60.4 us -> 15.2 us
  local copies, waits for them, and re-layouts: 19 us -> 13.5 us
    all_gather x2 -> x1, waiting for transfers between devices: 51.6 us -> 6.26 us  [local(): all_tokens = lax.all_gather(tokens, ('lon', 'lat'), axis=0, tiled=True)]
    all_gather x2 -> x0, local copies, waits for them, and re-layouts: 3.78 us -> none  [the longest x1 2.26 us: local(): lax.all_gather(value_rows, ('lon', 'lat'), axis=0, tiled=True)]
    dot_general x1, matrix products: 1.01 us -> 2.66 us  [local(): jnp.dot(all_normed, keyvalue_weight, preferred_element_type=jnp.float32)]
    dot_general x1, matrix products: 1.91 us -> 0.44 us  [local(): jnp.einsum('hts,shd->thd', weights.astype(jnp.bfloat16), value_heads, pre...]
    reduce_sum x4 -> x5, other arithmetic: 5.57 us -> 6.38 us  [rescale_rows(): jnp.mean(matrix * matrix, axis=-1, keepdims=True) + 1e-06]
    unnamed x18 -> x20, local copies, waits for them, and re-layouts: 5.14 us -> 5.15 us
  transfers between devices with their start and end apart: 10 -> 9, of which waited for: 7 -> 5; matrix products, arithmetic and copies ran while one was open for 25% -> 29% of each run, Pallas kernels for 0% -> 0%
where the time goes in v1:
time: 96.5 us; the launch traced here: 96 us
  other arithmetic  19.1 us (20%)
  matrix products  18 us (19%)
  starting transfers between devices  15.6 us (16%)
  waiting for transfers between devices  15.2 us (16%)
  between operations  14.4 us (15%)
  local copies, waits for them, and re-layouts  13.5 us (14%)
    conv_general_dilated x2, matrix products, convolve(): lax.conv_general_dilated(padded[None], kernel, (1, 1), 'VALID', dimension...  11.6 us
    ppermute x4, starting transfers between devices, padded_2(): lax.ppermute(lax.slice_in_dim(block, block.shape[dim] - width, None, axis...  9.06 us
    ppermute x4, waiting for transfers between devices, padded_2(): lax.ppermute(lax.slice_in_dim(block, 0, width, axis=dim), axis, backward)  7.09 us
    ppermute x4, starting transfers between devices, padded_2(): lax.ppermute(lax.slice_in_dim(block, 0, width, axis=dim), axis, backward)  6.52 us
    reduce_sum x5, other arithmetic, rescale_rows(): jnp.mean(matrix * matrix, axis=-1, keepdims=True) + 1e-06  6.38 us
    all_gather x1, waiting for transfers between devices, local(): all_tokens = lax.all_gather(tokens, ('lon', 'lat'), axis=0, tiled=True)  6.26 us
    unnamed x20, local copies, waits for them, and re-layouts  5.15 us
    conv_general_dilated x6, local copies, waits for them, and re-layouts, convolve(): lax.conv_general_dilated(padded[None], kernel, (1, 1), 'VALID', dimension...  4.81 us
  transfers between devices with their start and end apart: 9, of which 5 were waited for; matrix products, arithmetic and copies ran while one was open for 29% of the time, Pallas kernels for 0%

profile of v1, /device:TPU:0, one launch (start us, length us, event | category | flops | bytes accessed | tf_op | source)
XLA Modules:
  0.0 96.0 jit_solution(14286694379610430655)
XLA Ops:
  7.2 0.0 copy-start
  7.2 0.0 all-gather.2.cloned.1.call-start
  7.2 0.8 slice_bitcast_fusion.4
  8.0 3.4 %fusion.2 = f32[128,64]{0,1:T(8,128)S(1)} fusion(bf16[128,64,128]{2,1,0:T(8,128)(2,1)} %param.10), kind=kLoop, calls=%fused_computation.6 | loop fusion | flops 3137536 | bytes 2129920 | tf_op jit(solution)/shard_map/reduce_sum | solution.py:25
  11.4 3.4 %fusion.9 = bf16[128,64,128]{2,0,1:T(8,128)(2,1)S(1)} fusion(f32[128]{0:T(128)S(1)} %get-tuple-element.13, f32[128,64]{0,1:T(8,128)S(1)} %add_rsqrt_fusion.2, bf16[128,64,128]{2,1,0:T(8,128)(2,1)} %param.10), kind=kLoop, calls=%fused_computation.13 | loop fusion | flops 8388608 | bytes 4227584 | tf_op jit(solution)/shard_map/convert_element_type | solution.py:67
  14.9 0.1 fusion.63
  14.9 0.5 collective-permute-start
  15.4 2.0 %collective-permute-start.1 = (bf16[1,64,128]{2,0,1:T(2,128)(2,1)S(1)}, bf16[1,64,128]{2,0,1:T(2,128)(2,1)S(1)}, u32[]{:S(2)}, u32[]{:S(2)}) collective-permute-start(bf16[1,64,128]{2,0,1:T(2,128)(2,1)S(1)} %get-tuple-element.11), channel_id=1, source_target_pairs={{8,0},{16,8},{24,16},{0,24},{9,1},{17,9},{25,17},{1,25},{10,2},{18... | collective-permute-start | bytes 49160 | tf_op jit(solution)/shard_map/ppermute | solution.py:19
  17.4 0.6 reshape.92
  18.1 0.0 all-gather.2.cloned.1.call-update
  18.1 0.1 fusion.49
  18.2 0.1 fusion.51
  18.3 2.0 %copy.20 = bf16[512,512]{0,1:T(8,128)(2,1)} copy(bf16[512,512]{1,0:T(8,128)(2,1)} %param.16) | data formatting | bytes 1048576 | tf_op args[6]
  20.4 0.0 collective-permute-done
  20.4 0.0 collective-permute-done.1
  20.4 4.1 %collective-permute-start.2 = (bf16[130,1,128]{2,0,1:T(8,128)(2,1)S(1)}, bf16[130,1,128]{2,0,1:T(8,128)(2,1)S(1)}, u32[]{:S(2)}, u32[]{:S(2)}) collective-permute-start(bf16[130,1,128]{2,0,1:T(8,128)(2,1)S(1)} %get-tuple-element.6), channel_id=1, source_target_pairs={{0,1},{1,2},{2,3},{3,4},{4,5},{5,6},{6,7},{8,9},{9,10},{10,11},{11... | collective-permute-start | bytes 99848 | tf_op jit(solution)/shard_map/ppermute | solution.py:16
  24.6 1.5 %collective-permute-start.3 = (bf16[130,1,128]{2,0,1:T(8,128)(2,1)S(1)}, bf16[130,1,128]{2,0,1:T(8,128)(2,1)S(1)}, u32[]{:S(2)}, u32[]{:S(2)}) collective-permute-start(bf16[130,1,128]{2,0,1:T(8,128)(2,1)S(1)} %get-tuple-element.7), channel_id=1, source_target_pairs={{1,0},{2,1},{3,2},{4,3},{5,4},{6,5},{7,6},{9,8},{10,9},{11,10},{12... | collective-permute-start | bytes 99848 | tf_op jit(solution)/shard_map/ppermute | solution.py:19
  26.0 1.5 %multiply_reduce_fusion.2 = (f32[32,8]{0,1:T(8,128)S(1)}, f32[32,8,64]{2,0,1:T(8,128)S(1)}) fusion(bf16[32,512,1]{1,0,2:T(8,128)(2,1)S(1)} %reshape.124, bf16[8,64,512]{2,1,0:T(8,128)(2,1)} %bitcast.73), kind=kOutput, calls=%fused_computation.63 | convolution fusion | flops 16809728 | bytes 623616 | tf_op jit(solution)/shard_map/dot_general | solution.py:78
  27.5 0.0 collective-permute-done.2
  27.5 2.9 %collective-permute-done.3 = bf16[130,1,128]{2,0,1:T(8,128)(2,1)S(1)} collective-permute-done((bf16[130,1,128]{2,0,1:T(8,128)(2,1)S(1)}, bf16[130,1,128]{2,0,1:T(8,128)(2,1)S(1)}, u32[]{:S(2)}, u32[]{:S(2)}) %collective-permute-start.3) | collective-permute-done | bytes 33312 | tf_op jit(solution)/shard_map/ppermute | solution.py:19
  30.4 1.7 %maximum_bitcast_fusion = bf16[130,1,66,128]{3,0,2,1:T(8,128)(2,1)S(1)} fusion(bf16[130,1,128]{2,0,1:T(8,128)(2,1)S(1)} %collective-permute-done.3, bf16[1,64,128]{2,0,1:T(2,128)(2,1)S(1)} %collective-permute-done.1, bf16[128,64,128]{2,0,1:T(8,128)(2,1)S(1)} %fusion.9, bf16[1,64,128]{2,0,1:T(2,128)(2,1)S(1)} %collective-permute-done, ...), kind=kLoop, calls=%fused_computation.36 | loop fusion | flops 10982400 | bytes 4392960 | tf_op jit(solution)/shard_map/broadcast_in_dim | solution.py:35
  32.1 0.0 copy-start.7
  32.1 0.0 copy-start.8
  32.2 0.2 pad
  32.4 0.3 copy.15
  32.7 0.1 slice.71
  32.8 0.4 copy-done.7
  33.2 5.7 %broadcast_select_fusion.1 = f32[128,8,9,128]{3,1,2,0:T(8,128)S(1)} fusion(pred[8,9]{0,1:T(8,128)(4,1)S(1)} %copy-done.8, bf16[130,1,7,2,128]{4,2,3,0,1:T(8,128)(2,1)S(1)} %slice.71, bf16[130,1,8,9,128]{4,2,3,0,1:T(8,128)(2,1)S(1)} %copy.15, bf16[2,3,3,128,128]{4,3,2,1,0:T(8,128)(2,1)S(1)} %copy-done.7), kind=kOutput, calls=%fused_computation.35 | convolution fusion | flops 2727874560 | bytes 7944192 | tf_op jit(solution)/shard_map/conv_general_dilated | solution.py:34
  38.9 0.9 copy.16
  39.8 1.2 %multiply_reduce_fusion = f32[128,64]{0,1:T(8,128)S(1)} fusion(f32[128,1,72,128]{3,0,2,1:T(8,128)S(1)} %bitcast.66), kind=kLoop, calls=%fused_computation.19 | loop fusion | flops 2088960 | bytes 4227072 | tf_op jit(solution)/shard_map/reduce_sum | solution.py:25
  41.0 0.0 copy-start.6
  41.0 1.5 %multiply_convert_fusion = bf16[128,64,128]{2,0,1:T(8,128)(2,1)S(1)} fusion(f32[128,1,72,128]{3,0,2,1:T(8,128)S(1)} %bitcast.67, f32[128]{0:T(128)S(1)} %get-tuple-element.12, f32[128,64]{0,1:T(8,128)S(1)} %add_rsqrt_fusion.1), kind=kLoop, calls=%fused_computation.18 | loop fusion | flops 7340032 | bytes 6324736 | tf_op jit(solution)/shard_map/convert_element_type | solution.py:71
  42.5 0.1 fusion.62
  42.6 0.1 collective-permute-start.4
  42.6 1.7 %collective-permute-start.5 = (bf16[1,64,128]{2,0,1:T(2,128)(2,1)S(1)}, bf16[1,64,128]{2,0,1:T(2,128)(2,1)S(1)}, u32[]{:S(2)}, u32[]{:S(2)}) collective-permute-start(bf16[1,64,128]{2,0,1:T(2,128)(2,1)S(1)} %get-tuple-element.9), channel_id=1, source_target_pairs={{8,0},{16,8},{24,16},{0,24},{9,1},{17,9},{25,17},{1,25},{10,2},{18... | collective-permute-start | bytes 49160 | tf_op jit(solution)/shard_map/ppermute | solution.py:19
  44.4 1.6 %collective-permute-done.4 = bf16[1,64,128]{2,0,1:T(2,128)(2,1)S(1)} collective-permute-done((bf16[1,64,128]{2,0,1:T(2,128)(2,1)S(1)}, bf16[1,64,128]{2,0,1:T(2,128)(2,1)S(1)}, u32[]{:S(2)}, u32[]{:S(2)}) %collective-permute-start.4) | collective-permute-done | bytes 16416 | tf_op jit(solution)/shard_map/ppermute | solution.py:16
  45.9 0.0 collective-permute-done.5
  46.0 4.4 %collective-permute-start.6 = (bf16[130,1,128]{2,0,1:T(8,128)(2,1)S(1)}, bf16[130,1,128]{2,0,1:T(8,128)(2,1)S(1)}, u32[]{:S(2)}, u32[]{:S(2)}) collective-permute-start(bf16[130,1,128]{2,0,1:T(8,128)(2,1)S(1)} %get-tuple-element.4), channel_id=1, source_target_pairs={{0,1},{1,2},{2,3},{3,4},{4,5},{5,6},{6,7},{8,9},{9,10},{10,11},{11... | collective-permute-start | bytes 99848 | tf_op jit(solution)/shard_map/ppermute | solution.py:16
  50.4 1.3 %collective-permute-start.7 = (bf16[130,1,128]{2,0,1:T(8,128)(2,1)S(1)}, bf16[130,1,128]{2,0,1:T(8,128)(2,1)S(1)}, u32[]{:S(2)}, u32[]{:S(2)}) collective-permute-start(bf16[130,1,128]{2,0,1:T(8,128)(2,1)S(1)} %get-tuple-element.5), channel_id=1, source_target_pairs={{1,0},{2,1},{3,2},{4,3},{5,4},{6,5},{7,6},{9,8},{10,9},{11,10},{12... | collective-permute-start | bytes 99848 | tf_op jit(solution)/shard_map/ppermute | solution.py:19
  51.7 0.3 collective-permute-done.6
  52.0 4.2 %collective-permute-done.7 = bf16[130,1,128]{2,0,1:T(8,128)(2,1)S(1)} collective-permute-done((bf16[130,1,128]{2,0,1:T(8,128)(2,1)S(1)}, bf16[130,1,128]{2,0,1:T(8,128)(2,1)S(1)}, u32[]{:S(2)}, u32[]{:S(2)}) %collective-permute-start.7) | collective-permute-done | bytes 33312 | tf_op jit(solution)/shard_map/ppermute | solution.py:19
  56.2 2.0 %maximum_bitcast_fusion.1 = bf16[130,1,66,128]{3,0,2,1:T(8,128)(2,1)S(1)} fusion(bf16[130,1,128]{2,0,1:T(8,128)(2,1)S(1)} %collective-permute-done.7, bf16[1,64,128]{2,0,1:T(2,128)(2,1)S(1)} %collective-permute-done.5, bf16[128,64,128]{2,0,1:T(8,128)(2,1)S(1)} %multiply_convert_fusion, bf16[1,64,128]{2,0,1:T(2,128)(2,1)S(1)} %collective-permute-done.4, ...), kind=kLoop, calls=%fused_computation.37 | loop fusion | flops 10982400 | bytes 4392960 | tf_op jit(solution)/shard_map/broadcast_in_dim | solution.py:35
  58.2 0.2 pad.2
  58.4 0.3 copy.18
  58.7 0.1 slice.75
  58.8 5.9 %broadcast_select_fusion = f32[128,8,9,128]{3,1,2,0:T(8,128)S(1)} fusion(pred[8,9]{0,1:T(8,128)(4,1)S(1)} %copy-done.8, bf16[130,1,7,2,128]{4,2,3,0,1:T(8,128)(2,1)S(1)} %slice.75, bf16[130,1,8,9,128]{4,2,3,0,1:T(8,128)(2,1)S(1)} %copy.18, bf16[2,3,3,128,128]{4,3,2,1,0:T(8,128)(2,1)S(1)} %copy-done.7), kind=kOutput, calls=%fused_computation.34 | convolution fusion | flops 2727874560 | bytes 7944192 | tf_op jit(solution)/shard_map/conv_general_dilated | solution.py:34
  64.7 3.0 %copy.19 = f32[128,8,9,128]{3,0,2,1:T(8,128)} copy(f32[128,8,9,128]{3,1,2,0:T(8,128)S(1)} %broadcast_select_fusion) | data formatting | bytes 9437184 | tf_op jit(solution)/shard_map/conv_general_dilated | solution.py:34
  67.7 6.3 %all-gather.2.cloned.1.call-done = bf16[1024,512]{1,0:T(8,128)(2,1)} async-done(((bf16[32,512]{1,0:T(8,128)(2,1)}), bf16[1024,512]{1,0:T(8,128)(2,1)}) %all-gather.2.cloned.1.call-update) | async-done | bytes 1048592 | tf_op jit(solution)/shard_map/all_gather | solution.py:82
  74.0 1.5 %fusion.26 = f32[1024]{0:T(1024)S(1)} fusion(bf16[1024,512]{1,0:T(8,128)(2,1)} %all-gather.2.cloned.1.call-done), kind=kLoop, calls=%fused_computation.38 | loop fusion | flops 1571840 | bytes 1052672 | tf_op jit(solution)/shard_map/reduce_sum | solution.py:25
  75.5 2.7 %fusion.38 = f32[1024,1024]{0,1:T(8,128)S(1)} fusion(bf16[512,1024]{1,0:T(8,128)(2,1)S(1)} %copy-done, bf16[1024,512]{1,0:T(8,128)(2,1)} %all-gather.2.cloned.1.call-done, f32[512]{0:T(512)S(1)} %copy-done.5, f32[1024]{0:T(1024)S(1)} %add_rsqrt_fusion.5), kind=kOutput, calls=%fused_computation.52 | convolution fusion | flops 1075838976 | bytes 6297600 | tf_op jit(solution)/shard_map/dot_general | solution.py:84
  78.2 0.2 slice.78
  78.4 0.0 copy-start.2
  78.4 0.3 multiply_reduce_fusion.1
  78.7 0.0 copy-start.4
  78.7 0.2 slice.101
  78.9 0.5 fusion.64
  79.4 0.4 fusion.36
  79.9 0.1 convert_element_type.65
  80.0 1.3 %fusion.37 = bf16[32,512]{1,0:T(8,128)(2,1)S(1)} fusion(bf16[32,512]{1,0:T(8,128)(2,1)S(1)} %convert_element_type.65, bf16[512,512]{1,0:T(8,128)(2,1)} %param.18, bf16[32,512]{1,0:T(8,128)(2,1)S(1)} %copy-done.2), kind=kOutput, calls=%fused_computation.51 | convolution fusion | flops 16826368 | bytes 622592 | tf_op jit(solution)/shard_map/dot_general | solution.py:112
  81.3 0.6 reshape.95
  81.9 0.1 fusion.65
  82.1 0.5 add.101
  82.6 3.9 %fusion.11 = bf16[128,64,128]{2,0,1:T(8,128)(2,1)S(1)} fusion(f32[128,64,128]{2,0,1:T(8,128)S(1)} %bitcast.69, f32[128,1,72,128]{3,0,2,1:T(8,128)} %bitcast.68, bf16[128,64,128]{2,1,0:T(8,128)(2,1)S(1)} %copy-done.1), kind=kLoop, calls=%fused_computation.15 | loop fusion | flops 4194304 | bytes 12582912 | tf_op jit(solution)/shard_map/convert_element_type | solution.py:120
  86.5 2.7 %copy.23 = bf16[128,64,128]{2,1,0:T(8,128)(2,1)} copy(bf16[128,64,128]{2,0,1:T(8,128)(2,1)S(1)} %fusion.11) | data formatting | bytes 4194304
  (23 shorter events, 0.2 us)
Async XLA Ops:
  7.2 68.3 %copy-start = (bf16[512,1024]{1,0:T(8,128)(2,1)S(1)}, bf16[512,1024]{1,0:T(8,128)(2,1)}, u32[]{:S(2)}) copy-start(bf16[512,1024]{1,0:T(8,128)(2,1)} %param.17) | copy-start | bytes 3145732
  7.2 10.3 %copy-start.3 = (bf16[8,4,512]{2,1,0:T(4,128)(2,1)S(1)}, bf16[8,4,512]{2,1,0:T(4,128)(2,1)}, u32[]{:S(2)}) copy-start(bf16[8,4,512]{2,1,0:T(4,128)(2,1)} %param.11) | copy-start | bytes 98308
  7.2 11.0 %copy-start.5 = (f32[512]{0:T(512)S(1)}, f32[512]{0:T(512)}, u32[]{:S(2)}) copy-start(f32[512]{0:T(512)} %param.14) | copy-start | bytes 6148
  7.2 66.8 %all-gather.2.cloned.1.call-start = ((), (), s32[]{:S(2)}) async-start(), calls=%async_computation | async-start | bytes 1081344 | tf_op jit(solution)/shard_map/all_gather | solution.py:82
  14.9 5.5 %collective-permute-start = (bf16[1,64,128]{2,0,1:T(2,128)(2,1)S(1)}, bf16[1,64,128]{2,0,1:T(2,128)(2,1)S(1)}, u32[]{:S(2)}, u32[]{:S(2)}) collective-permute-start(bf16[1,64,128]{2,0,1:T(2,128)(2,1)S(1)} %get-tuple-element.10), channel_id=1, source_target_pairs={{0,8},{8,16},{16,24},{24,0},{1,9},{9,17},{17,25},{25,1},{2,10},{10... | collective-permute-start | bytes 49160 | tf_op jit(solution)/shard_map/ppermute | solution.py:16
  15.4 5.0 %collective-permute-start.1 = (bf16[1,64,128]{2,0,1:T(2,128)(2,1)S(1)}, bf16[1,64,128]{2,0,1:T(2,128)(2,1)S(1)}, u32[]{:S(2)}, u32[]{:S(2)}) collective-permute-start(bf16[1,64,128]{2,0,1:T(2,128)(2,1)S(1)} %get-tuple-element.11), channel_id=1, source_target_pairs={{8,0},{16,8},{24,16},{0,24},{9,1},{17,9},{25,17},{1,25},{10,2},{18... | collective-permute-start | bytes 49160 | tf_op jit(solution)/shard_map/ppermute | solution.py:19
  20.4 7.1 %collective-permute-start.2 = (bf16[130,1,128]{2,0,1:T(8,128)(2,1)S(1)}, bf16[130,1,128]{2,0,1:T(8,128)(2,1)S(1)}, u32[]{:S(2)}, u32[]{:S(2)}) collective-permute-start(bf16[130,1,128]{2,0,1:T(8,128)(2,1)S(1)} %get-tuple-element.6), channel_id=1, source_target_pairs={{0,1},{1,2},{2,3},{3,4},{4,5},{5,6},{6,7},{8,9},{9,10},{10,11},{11... | collective-permute-start | bytes 99848 | tf_op jit(solution)/shard_map/ppermute | solution.py:16
  24.6 5.8 %collective-permute-start.3 = (bf16[130,1,128]{2,0,1:T(8,128)(2,1)S(1)}, bf16[130,1,128]{2,0,1:T(8,128)(2,1)S(1)}, u32[]{:S(2)}, u32[]{:S(2)}) collective-permute-start(bf16[130,1,128]{2,0,1:T(8,128)(2,1)S(1)} %get-tuple-element.7), channel_id=1, source_target_pairs={{1,0},{2,1},{3,2},{4,3},{5,4},{6,5},{7,6},{9,8},{10,9},{11,10},{12... | collective-permute-start | bytes 99848 | tf_op jit(solution)/shard_map/ppermute | solution.py:19
  32.1 1.1 %copy-start.7 = (bf16[2,3,3,128,128]{4,3,2,1,0:T(8,128)(2,1)S(1)}, bf16[2,3,3,128,128]{4,3,2,1,0:T(8,128)(2,1)}, u32[]{:S(2)}) copy-start(bf16[2,3,3,128,128]{4,3,2,1,0:T(8,128)(2,1)} %param.13) | copy-start | bytes 1769476
  32.1 1.1 %copy-start.8 = (pred[8,9]{0,1:T(8,128)(4,1)S(1)}, pred[8,9]{0,1:T(8,128)(4,1)}, u32[]{:S(2)}) copy-start(pred[8,9]{0,1:T(8,128)(4,1)} %constant.37) | copy-start | bytes 220
  41.0 10.7 %copy-start.6 = (f32[2,64]{1,0:T(2,128)S(1)}, f32[2,64]{1,0:T(2,128)}, u32[]{:S(2)}) copy-start(f32[2,64]{1,0:T(2,128)} %param.15) | copy-start | bytes 1540
  42.6 3.4 %collective-permute-start.4 = (bf16[1,64,128]{2,0,1:T(2,128)(2,1)S(1)}, bf16[1,64,128]{2,0,1:T(2,128)(2,1)S(1)}, u32[]{:S(2)}, u32[]{:S(2)}) collective-permute-start(bf16[1,64,128]{2,0,1:T(2,128)(2,1)S(1)} %get-tuple-element.8), channel_id=1, source_target_pairs={{0,8},{8,16},{16,24},{24,0},{1,9},{9,17},{17,25},{25,1},{2,10},{10... | collective-permute-start | bytes 49160 | tf_op jit(solution)/shard_map/ppermute | solution.py:16
  42.6 3.3 %collective-permute-start.5 = (bf16[1,64,128]{2,0,1:T(2,128)(2,1)S(1)}, bf16[1,64,128]{2,0,1:T(2,128)(2,1)S(1)}, u32[]{:S(2)}, u32[]{:S(2)}) collective-permute-start(bf16[1,64,128]{2,0,1:T(2,128)(2,1)S(1)} %get-tuple-element.9), channel_id=1, source_target_pairs={{8,0},{16,8},{24,16},{0,24},{9,1},{17,9},{25,17},{1,25},{10,2},{18... | collective-permute-start | bytes 49160 | tf_op jit(solution)/shard_map/ppermute | solution.py:19
  46.0 6.0 %collective-permute-start.6 = (bf16[130,1,128]{2,0,1:T(8,128)(2,1)S(1)}, bf16[130,1,128]{2,0,1:T(8,128)(2,1)S(1)}, u32[]{:S(2)}, u32[]{:S(2)}) collective-permute-start(bf16[130,1,128]{2,0,1:T(8,128)(2,1)S(1)} %get-tuple-element.4), channel_id=1, source_target_pairs={{0,1},{1,2},{2,3},{3,4},{4,5},{5,6},{6,7},{8,9},{9,10},{10,11},{11... | collective-permute-start | bytes 99848 | tf_op jit(solution)/shard_map/ppermute | solution.py:16
  50.4 5.8 %collective-permute-start.7 = (bf16[130,1,128]{2,0,1:T(8,128)(2,1)S(1)}, bf16[130,1,128]{2,0,1:T(8,128)(2,1)S(1)}, u32[]{:S(2)}, u32[]{:S(2)}) collective-permute-start(bf16[130,1,128]{2,0,1:T(8,128)(2,1)S(1)} %get-tuple-element.5), channel_id=1, source_target_pairs={{1,0},{2,1},{3,2},{4,3},{5,4},{6,5},{7,6},{9,8},{10,9},{11,10},{12... | collective-permute-start | bytes 99848 | tf_op jit(solution)/shard_map/ppermute | solution.py:19
  78.4 1.6 %copy-start.2 = (bf16[32,512]{1,0:T(8,128)(2,1)S(1)}, bf16[32,512]{1,0:T(8,128)(2,1)}, u32[]{:S(2)}) copy-start(bf16[32,512]{1,0:T(8,128)(2,1)} %reshape.92) | copy-start | bytes 98308
  78.7 3.2 %copy-start.4 = (bf16[512,128]{1,0:T(8,128)(2,1)S(1)}, bf16[512,128]{1,0:T(8,128)(2,1)}, u32[]{:S(2)}) copy-start(bf16[512,128]{1,0:T(8,128)(2,1)} %param.19) | copy-start | bytes 393220
  79.4 3.1 %copy-start.1 = (bf16[128,64,128]{2,1,0:T(8,128)(2,1)S(1)}, bf16[128,64,128]{2,1,0:T(8,128)(2,1)}, u32[]{:S(2)}) copy-start(bf16[128,64,128]{2,1,0:T(8,128)(2,1)} %param.10) | copy-start | bytes 6291460
Sparse Core Ops, SparseCore 0:
  18.2 55.7 all-gather.1

commit v2 on v0

v2 whole, which is shorter than its diff:
```python
import functools
import math

import jax
import jax.numpy as jnp
from jax import lax
from jax.experimental import pallas as pl
from jax.experimental.pallas import tpu as pltpu
from jax.sharding import PartitionSpec as P

MESH = pl.DeviceIdType.MESH
F32 = jnp.float32
BF16 = jnp.bfloat16
LEFT = 8


def mm(a, b):
    return jnp.dot(a, b, preferred_element_type=F32)


def block_ones(size, block, value):
    r = lax.broadcasted_iota(jnp.int32, (size, size), 0) // block
    c = lax.broadcasted_iota(jnp.int32, (size, size), 1) // block
    return jnp.where(r == c, value, 0.0).astype(BF16)


def silu(v):
    half = 0.5 * v
    return half + half * jnp.tanh(half)


def norm_silu(x, ones, gain):
    flat = x.reshape(-1, x.shape[-1])
    ms = mm((flat * flat).astype(BF16), ones)
    return silu(flat * lax.rsqrt(ms + 1e-6) * gain).reshape(x.shape)


def chunk_of(total, most):
    return max(d for d in range(1, most + 1) if total % d == 0)


def body(
    lon_n,
    lat_n,
    fine_hbm,
    coarse_hbm,
    norm_gains,
    kernels_hbm,
    token_gain,
    head_gains,
    wq_hbm,
    wkv_hbm,
    wo_hbm,
    we_hbm,
    out_hbm,
    coarse_out,
    fine,
    h1,
    h2,
    x,
    w,
    wq,
    wkv,
    wo,
    we,
    tok,
    lift,
    outs,
    halo,
    cols_s,
    cols_r,
    cols2_s,
    cols2_r,
    dma,
    wsem,
    osem,
    hs,
    hr,
    c2s,
    c2r,
    ts,
    tr,
):
    pairs, _, width, ch = fine.shape
    rows = 2 * pairs
    own, wide = coarse_hbm.shape
    lon, lat = lax.axis_index("lon"), lax.axis_index("lat")
    up, down = lax.rem(lon + lon_n - 1, lon_n), lax.rem(lon + 1, lon_n)
    west, east = lax.rem(lat + lat_n - 1, lat_n), lax.rem(lat + 1, lat_n)
    has_west, has_east = lat > 0, lat < lat_n - 1

    steps = []
    d = lat_n // 2
    while d:
        steps.append((lon, lat + d - 2 * d * ((lat // d) % 2)))
        d //= 2
    d = lon_n // 2
    while d:
        steps.append((lon + d - 2 * d * ((lon // d) % 2), lat))
        d //= 2

    local = [
        pltpu.make_async_copy(coarse_hbm, tok.at[pl.ds(0, own)], dma.at[0]),
        pltpu.make_async_copy(fine_hbm, fine, dma.at[1]),
        pltpu.make_async_copy(wq_hbm, wq, dma.at[2]),
        pltpu.make_async_copy(wkv_hbm, wkv, dma.at[3]),
        pltpu.make_async_copy(wo_hbm, wo, dma.at[4]),
        pltpu.make_async_copy(we_hbm, we, dma.at[5]),
    ]
    taps = []
    for conv in range(2):
        for r in range(2):
            for a in range(3):
                taps.append(
                    pltpu.make_async_copy(
                        kernels_hbm.at[conv, a],
                        w.at[conv, a + r, :, :, pl.ds(r * ch, ch)],
                        wsem.at[len(taps)],
                    )
                )
    local[0].start()
    local[1].start()
    for copy in taps:
        copy.start()
    for copy in local[2:]:
        copy.start()

    cols_r[...] = jnp.zeros_like(cols_r)
    cols2_r[...] = jnp.zeros_like(cols2_r)
    barrier = pltpu.get_barrier_semaphore()
    ring = [(i, j) for i in (up, lon, down) for j in (west, lat, east)]
    del ring[4]
    for device in ring + steps:
        pl.semaphore_signal(barrier, inc=1, device_id=device, device_id_type=MESH)

    zero = jnp.zeros((3, ch, ch), BF16)
    for conv in range(2):
        w[conv, 3, :, :, pl.ds(0, ch)] = zero
        w[conv, 0, :, :, pl.ds(ch, ch)] = zero
    ones = block_ones(ch, ch, 1.0 / ch)
    ones2 = block_ones(2 * ch, ch, 1.0 / ch)

    pl.semaphore_wait(barrier, len(ring) + len(steps))

    def step_copy(s):
        size = own << s
        return pltpu.make_async_remote_copy(
            src_ref=tok.at[pl.ds(0, size)],
            dst_ref=tok.at[pl.ds(size, size)],
            send_sem=ts.at[s],
            recv_sem=tr.at[s],
            device_id=steps[s],
            device_id_type=MESH,
        )

    state = {"at": 0}

    def advance():
        s = state["at"]
        if s < len(steps):
            step_copy(s).wait()
            if s + 1 < len(steps):
                step_copy(s + 1).start()
            state["at"] = s + 1

    local[0].wait()
    step_copy(0).start()

    def remote(src, dst, at, device):
        return pltpu.make_async_remote_copy(
            src_ref=src,
            dst_ref=dst,
            send_sem=hs.at[at],
            recv_sem=hr.at[at],
            device_id=device,
            device_id_type=MESH,
        )

    to_down = remote(fine_hbm.at[pl.ds(pairs - 1, 1)], halo.at[pl.ds(0, 1)], 0, (down, lat))
    to_up = remote(fine_hbm.at[pl.ds(0, 1)], halo.at[pl.ds(1, 1)], 1, (up, lat))
    to_down.start()
    to_up.start()

    local[1].wait()
    cols_s[0] = fine[:, :, 0:16, :].astype(F32)[:, :, 0:1, :]
    cols_s[1] = fine[:, :, width - 16 : width, :].astype(F32)[:, :, 15:16, :]
    side_copies = []
    for side, (there, ok_send) in enumerate(((west, has_west), (east, has_east))):
        got = cols_r.at[1 - side]
        mine = cols_s.at[side]
        side_copies.append(
            [
                remote(mine, got.at[pl.ds(1, pairs)], 2 + side * 3, (lon, there)),
                remote(
                    mine.at[pl.ds(pairs - 1, 1)],
                    got.at[pl.ds(0, 1)],
                    3 + side * 3,
                    (down, there),
                ),
                remote(
                    mine.at[pl.ds(0, 1)],
                    got.at[pl.ds(pairs + 1, 1)],
                    4 + side * 3,
                    (up, there),
                ),
            ]
        )

    def start_side(side):
        for copy in side_copies[side]:
            copy.start()

    pl.when(has_west)(lambda: start_side(0))
    pl.when(has_east)(lambda: start_side(1))

    gain0 = norm_gains[0:1, :]
    gain1 = norm_gains[1:2, :]
    n0 = chunk_of(pairs, 4)

    def first(i, c):
        at = pl.multiple_of(i * n0, n0)
        v = fine[pl.ds(at, n0)].astype(F32)
        h1[pl.ds(at + 1, n0), :, LEFT : LEFT + width, :] = norm_silu(v, ones, gain0)
        return c

    lax.fori_loop(0, pairs // n0, first, 0)
    advance()

    to_down.wait()
    to_up.wait()
    v = halo[...].astype(F32)
    v = norm_silu(v, ones, gain0)
    h1[0:1, :, LEFT : LEFT + width, :] = v[0:1]
    h1[pairs + 1 : pairs + 2, :, LEFT : LEFT + width, :] = v[1:2]

    def wait_send(side):
        for copy in side_copies[side]:
            copy.wait_send()

    def wait_recv(side):
        for copy in side_copies[side]:
            copy.wait_recv()

    pl.when(has_west)(lambda: wait_send(0))
    pl.when(has_east)(lambda: wait_send(1))
    pl.when(has_east)(lambda: wait_recv(0))
    pl.when(has_west)(lambda: wait_recv(1))
    gain0c = gain0.reshape(1, 1, 1, ch)
    for side, at in ((0, LEFT - 1), (1, LEFT + width)):
        v = cols_r[side]
        ms = jnp.mean(v * v, axis=-1, keepdims=True)
        h1[:, :, at : at + 1, :] = silu(v * lax.rsqrt(ms + 1e-6) * gain0c)

    def pack(src, count):
        n = chunk_of(count, 3)

        def go(i, c):
            at = i * n
            for q in range(2):
                for b in range(3):
                    lo = LEFT - 1 + b
                    col = (q * 3 + b) * ch
                    x[pl.ds(at, n), :, col : col + ch] = src[
                        pl.ds(at, n), q, lo : lo + width, :
                    ].astype(BF16)
            return c

        lax.fori_loop(0, count // n, go, 0)

    pack(h1, pairs + 2)
    advance()
    for copy in taps:
        copy.wait()

    half_k = 6 * ch

    def conv(at, n, conv_at):
        wa = w[conv_at, 0:2].reshape(half_k, 2 * ch)
        wb = w[conv_at, 2:4].reshape(half_k, 2 * ch)
        a = x[pl.ds(at, n)].reshape(n * width, half_k)
        b = x[pl.ds(at + 1, n)].reshape(n * width, half_k)
        return mm(a, wa) + mm(b, wb)

    n1 = chunk_of(pairs + 1, 5)

    def second(i, c):
        at = i * n1
        y = conv(at, n1, 0)
        ms = mm((y * y).astype(BF16), ones2)
        z = y * lax.rsqrt(ms + 1e-6)
        for q in range(2):
            v = silu(z[:, q * ch : (q + 1) * ch] * gain1)
            h2[pl.ds(at, n1), q, LEFT : LEFT + width, :] = v.reshape(n1, width, ch)
        return c

    loops = (pairs + 1) // n1
    lax.fori_loop(0, loops // 2, second, 0)
    advance()
    lax.fori_loop(loops // 2, loops, second, 0)
    advance()

    cols2_s[0] = h2[:, :, LEFT : LEFT + 1, :]
    cols2_s[1] = h2[:, :, LEFT + width - 1 : LEFT + width, :]

    def remote2(side, there):
        return pltpu.make_async_remote_copy(
            src_ref=cols2_s.at[side],
            dst_ref=cols2_r.at[1 - side],
            send_sem=c2s.at[side],
            recv_sem=c2r.at[side],
            device_id=(lon, there),
            device_id_type=MESH,
        )

    to_west, to_east = remote2(0, west), remote2(1, east)
    pl.when(has_west)(to_west.start)
    pl.when(has_east)(to_east.start)

    for copy in local[2:]:
        copy.wait()
    heads = wide // head_gains.shape[1]
    hd = wide // heads
    tg = token_gain[...]
    gq = jnp.concatenate([head_gains[0:1, :]] * heads, axis=1)
    gk = jnp.concatenate([head_gains[1:2, :]] * heads, axis=1)
    per_head = block_ones(wide, hd, 1.0 / hd)

    def norm_tokens(t):
        return (t * lax.rsqrt(jnp.mean(t * t, axis=-1, keepdims=True) + 1e-6) * tg).astype(BF16)

    def norm_heads(v, g):
        return v * lax.rsqrt(mm((v * v).astype(BF16), per_head) + 1e-6) * g

    mine = tok[0:own].astype(F32)
    q = norm_heads(mm(norm_tokens(mine), wq[...]), gq) * (1.0 / math.sqrt(hd))
    r = lax.broadcasted_iota(jnp.int32, (heads * own, wide), 0) // own
    c = lax.broadcasted_iota(jnp.int32, (heads * own, wide), 1) // hd
    head_mask = r == c
    qb = jnp.where(head_mask, jnp.concatenate([q] * heads, axis=0), 0.0).astype(BF16)
    while state["at"] < len(steps):
        advance()
    total = own * lon_n * lat_n
    nt = min(256, total)

    def attend(i, carry):
        acc, tot = carry
        t = tok[pl.ds(pl.multiple_of(i * nt, nt), nt)].astype(F32)
        kv = mm(norm_tokens(t), wkv[...])
        k = norm_heads(kv[:, :wide], gk).astype(BF16)
        vv = kv[:, wide:].astype(BF16)
        s = lax.dot_general(qb, k, (((1,), (1,)), ((), ())), preferred_element_type=F32)
        e = jnp.exp(s)
        return acc + mm(e.astype(BF16), vv), tot + jnp.sum(e, axis=1, keepdims=True)

    acc, tot = lax.fori_loop(
        0,
        total // nt,
        attend,
        (jnp.zeros((heads * own, wide), F32), jnp.zeros((heads * own, 1), F32)),
    )
    att = jnp.where(head_mask, acc / tot, 0.0).reshape(heads, own, wide)
    att = jnp.sum(att, axis=0).astype(BF16)
    coarse = (mine + mm(att, wo[...])).astype(BF16)
    coarse_out[...] = coarse
    lon_t = lift.shape[0]
    lat_t = own // lon_t
    rr = lax.broadcasted_iota(jnp.int32, (lon_t * width, own), 0) // (width // lat_t)
    cc = lax.broadcasted_iota(jnp.int32, (lon_t * width, own), 1)
    rep = mm(jnp.where(rr == cc, 1.0, 0.0).astype(BF16), coarse).astype(BF16)
    lift[...] = mm(rep, we[...]).reshape(lon_t, width, ch)

    pl.when(has_west)(to_west.wait_send)
    pl.when(has_east)(to_east.wait_send)
    pl.when(has_east)(to_west.wait_recv)
    pl.when(has_west)(to_east.wait_recv)
    h2[:, :, LEFT - 1 : LEFT, :] = cols2_r[0]
    h2[:, :, LEFT + width : LEFT + width + 1, :] = cols2_r[1]
    pack(h2, pairs + 1)
    n2 = pairs // lon_t

    def out_copy(i):
        at = pl.multiple_of(i * n2, n2)
        return pltpu.make_async_copy(
            outs.at[pl.ds(at, n2)], out_hbm.at[pl.ds(at, n2)], osem.at[i]
        )

    def third(i, c):
        at = pl.multiple_of(i * n2, n2)
        y = conv(at, n2, 1)
        up_row = lift[i]
        for q in range(2):
            v = y[:, q * ch : (q + 1) * ch].reshape(n2, width, ch)
            outs[pl.ds(at, n2), q] = (
                fine[pl.ds(at, n2), q].astype(F32) + v + up_row[None]
            ).astype(BF16)
        out_copy(i).start()
        return c

    lax.fori_loop(0, lon_t, third, 0)
    for i in range(lon_t):
        out_copy(i).wait()


def local(lon_n, lat_n, fine_state, coarse_state, norm_gains, kernels, token_gain, head_gains,
          query_weight, keyvalue_weight, output_weight, expand_weight):
    rows, width, ch = fine_state.shape
    lon_t, lat_t, wide = coarse_state.shape
    pairs, own = rows // 2, lon_t * lat_t
    hops = int(math.log2(lon_n)) + int(math.log2(lat_n))
    any_, vm = pl.BlockSpec(memory_space=pl.ANY), pl.BlockSpec(memory_space=pltpu.VMEM)
    sem = pltpu.SemaphoreType.DMA
    fine_result, coarse_result = pl.pallas_call(
        functools.partial(body, lon_n, lat_n),
        out_shape=(
            jax.ShapeDtypeStruct((pairs, 2, width, ch), BF16),
            jax.ShapeDtypeStruct((own, wide), BF16),
        ),
        in_specs=[any_, any_, vm, any_, vm, vm, any_, any_, any_, any_],
        out_specs=(any_, vm),
        scratch_shapes=[
            pltpu.VMEM((pairs, 2, width, ch), BF16),
            pltpu.VMEM((pairs + 2, 2, width + 16, ch), F32),
            pltpu.VMEM((pairs + 1, 2, width + 16, ch), F32),
            pltpu.VMEM((pairs + 2, width, 6 * ch), BF16),
            pltpu.VMEM((2, 4, 3, ch, 2 * ch), BF16),
            pltpu.VMEM(query_weight.shape, BF16),
            pltpu.VMEM(keyvalue_weight.shape, BF16),
            pltpu.VMEM(output_weight.shape, BF16),
            pltpu.VMEM(expand_weight.shape, BF16),
            pltpu.VMEM((own * lon_n * lat_n, wide), BF16),
            pltpu.VMEM((lon_t, width, ch), F32),
            pltpu.VMEM((pairs, 2, width, ch), BF16),
            pltpu.VMEM((2, 2, width, ch), BF16),
            pltpu.VMEM((2, pairs, 2, 1, ch), F32),
            pltpu.VMEM((2, pairs + 2, 2, 1, ch), F32),
            pltpu.VMEM((2, pairs + 1, 2, 1, ch), F32),
            pltpu.VMEM((2, pairs + 1, 2, 1, ch), F32),
            sem((6,)),
            sem((12,)),
            sem((lon_t,)),
            sem((8,)),
            sem((8,)),
            sem((2,)),
            sem((2,)),
            sem((hops,)),
            sem((hops,)),
        ],
        compiler_params=pltpu.CompilerParams(
            collective_id=0, has_side_effects=True, vmem_limit_bytes=56 * 2**20
        ),
    )(
        fine_state.reshape(pairs, 2, width, ch),
        coarse_state.reshape(own, wide),
        norm_gains,
        kernels,
        token_gain.reshape(1, wide),
        head_gains,
        query_weight,
        keyvalue_weight,
        output_weight,
        expand_weight,
    )
    return fine_result.reshape(fine_state.shape), coarse_result.reshape(coarse_state.shape)


def solution(mesh):
    split = P("lon", "lat", None)
    return jax.shard_map(
        functools.partial(local, mesh.shape["lon"], mesh.shape["lat"]),
        mesh=mesh,
        in_specs=(split, split) + (P(),) * 8,
        out_specs=(split, split),
        check_vma=False,
    )
```

time: 146 us -> 45.9 us (0.31)
  waiting for transfers between devices: 60.4 us -> 0 us
  Pallas kernels: 0 us -> 39.1 us
  other arithmetic: 18.7 us -> 0 us
  matrix products: 17.5 us -> 0 us
  starting transfers between devices: 15.8 us -> 0 us
  between operations: 14.4 us -> 0.64 us
  local copies, waits for them, and re-layouts: 19 us -> 5.85 us
    all_gather x2 -> x0, waiting for transfers between devices: 51.6 us -> none  [the longest x1 51.6 us: local(): lax.all_gather(value_rows, ('lon', 'lat'), axis=0, tiled=True)]
    pallas_call x0 -> x1, Pallas kernels: none -> 39.1 us  [local(): pl.pallas_call(functools.partial(body, lon_n, lat_n), out_shape=(jax.Shap...]
    ppermute x8 -> x0, starting transfers between devices: 15.7 us -> none  [the longest x4 9.99 us: padded_2(): lax.ppermute(lax.slice_in_dim(block, block.shape[dim] - width, None, axis...]
    conv_general_dilated x2 -> x0, matrix products: 11.6 us -> none  [convolve(): lax.conv_general_dilated(padded[None], kernel, (1, 1), 'VALID', dimension...]
    convert_element_type x5 -> x0, other arithmetic: 9.53 us -> none  [the longest x1 3.9 us: local(): merged.reshape(lon_cells, lat_cells, channels).astype(jnp.bfloat16)]
    ppermute x8 -> x0, waiting for transfers between devices: 8.71 us -> none  [the longest x4 6.44 us: padded_2(): lax.ppermute(lax.slice_in_dim(block, 0, width, axis=dim), axis, backward)]
    dot_general x6 -> x0, matrix products: 5.88 us -> none  [the longest x1 1.91 us: local(): jnp.einsum('hts,shd->thd', weights.astype(jnp.bfloat16), value_heads, pre...]
    reduce_sum x4 -> x0, other arithmetic: 5.57 us -> none  [rescale_rows(): jnp.mean(matrix * matrix, axis=-1, keepdims=True) + 1e-06]
  transfers between devices with their start and end apart: 10 -> 0, of which waited for: 7 -> 0; matrix products, arithmetic and copies ran while one was open for 25% -> 0% of each run, Pallas kernels for 0% -> 0%
where the time goes in v2:
time: 45.9 us; the launch traced here: 45.6 us
  Pallas kernels  39.1 us (85%)
  local copies, waits for them, and re-layouts  5.85 us (13%)
  between operations  0.64 us (1%)
    pallas_call x1, Pallas kernels, local(): pl.pallas_call(functools.partial(body, lon_n, lat_n), out_shape=(jax.Shap...  39.1 us
    unnamed x1, local copies, waits for them, and re-layouts  3.08 us
    reshape x1, local copies, waits for them, and re-layouts, local(): coarse_result.reshape(coarse_state.shape)  1.39 us
    reshape x1, local copies, waits for them, and re-layouts, local(): coarse_state.reshape(own, wide)  1.39 us

profile of v2, /device:TPU:0, one launch (start us, length us, event | category | flops | bytes accessed | tf_op | source)
XLA Modules:
  0.0 45.6 jit_solution(10788733909975452698)
XLA Ops:
  0.6 1.4 %reshape.20.coarse_hbm = bf16[32,512]{1,0:T(8,128)(2,1)} reshape(bf16[8,4,512]{2,1,0:T(4,128)(2,1)} %param.11) | data formatting | bytes 65536 | tf_op jit(solution)/shard_map/reshape | solution.py:453
  2.0 39.1 %shard_map.113 = (bf16[64,2,64,128]{3,2,1,0:T(8,128)(2,1)}, bf16[32,512]{1,0:T(8,128)(2,1)}) custom-call(bf16[64,2,64,128]{3,2,1,0:T(8,128)(2,1)} %bitcast.3, bf16[32,512]{1,0:T(8,128)(2,1)} %reshape.20.coarse_hbm, f32[2,128]{1,0:T(2,128)} %norm_gains.1, bf16[2,3,3,128,128]{4,3,2,1,0:T(8,128)(2,1)} %kernels_hbm.1, f32[1,512]{1,0:T(1,128)} %bitcast.5, ...), custom_call_target="tpu_custom_call" | custom-call | tf_op jit(solution)/shard_map/pallas_call | solution.py:412
  41.1 1.4 %reshape.23 = bf16[8,4,512]{2,1,0:T(4,128)(2,1)} reshape(bf16[32,512]{1,0:T(8,128)(2,1)} %get-tuple-element.5) | data formatting | bytes 65536 | tf_op jit(solution)/shard_map/reshape | solution.py:463
  42.5 3.1 %copy.13 = bf16[128,64,128]{2,1,0:T(8,128)(2,1)} copy(bf16[128,64,128]{2,1,0:T(8,128)(2,1)} %bitcast.4) | data formatting | bytes 4194304

commit v3 on v2

--- a/solution.py
+++ b/solution.py
@@ -43,7 +43,7 @@
     lon_n,
     lat_n,
     fine_hbm,
-    coarse_hbm,
+    coarse_in,
     norm_gains,
     kernels_hbm,
     token_gain,
@@ -55,9 +55,10 @@
     out_hbm,
     coarse_out,
     fine,
-    h1,
-    h2,
-    x,
+    hb,
+    x1,
+    x2,
+    stage,
     w,
     wq,
     wkv,
@@ -83,7 +84,8 @@
 ):
     pairs, _, width, ch = fine.shape
     rows = 2 * pairs
-    own, wide = coarse_hbm.shape
+    lon_t, lat_t, wide = coarse_in.shape
+    own = lon_t * lat_t
     lon, lat = lax.axis_index("lon"), lax.axis_index("lat")
     up, down = lax.rem(lon + lon_n - 1, lon_n), lax.rem(lon + 1, lon_n)
     west, east = lax.rem(lat + lat_n - 1, lat_n), lax.rem(lat + 1, lat_n)
@@ -100,12 +102,11 @@
         d //= 2
 
     local = [
-        pltpu.make_async_copy(coarse_hbm, tok.at[pl.ds(0, own)], dma.at[0]),
-        pltpu.make_async_copy(fine_hbm, fine, dma.at[1]),
-        pltpu.make_async_copy(wq_hbm, wq, dma.at[2]),
-        pltpu.make_async_copy(wkv_hbm, wkv, dma.at[3]),
-        pltpu.make_async_copy(wo_hbm, wo, dma.at[4]),
-        pltpu.make_async_copy(we_hbm, we, dma.at[5]),
+        pltpu.make_async_copy(fine_hbm, fine, dma.at[0]),
+        pltpu.make_async_copy(wq_hbm, wq, dma.at[1]),
+        pltpu.make_async_copy(wkv_hbm, wkv, dma.at[2]),
+        pltpu.make_async_copy(wo_hbm, wo, dma.at[3]),
+        pltpu.make_async_copy(we_hbm, we, dma.at[4]),
     ]
     taps = []
     for conv in range(2):
@@ -118,21 +119,21 @@
                         wsem.at[len(taps)],
                     )
                 )
-    local[0].start()
-    local[1].start()
-    for copy in taps:
-        copy.start()
-    for copy in local[2:]:
+    for copy in local[:1] + taps + local[1:]:
         copy.start()
 
     cols_r[...] = jnp.zeros_like(cols_r)
     cols2_r[...] = jnp.zeros_like(cols2_r)
+    hb[...] = jnp.zeros_like(hb)
     barrier = pltpu.get_barrier_semaphore()
     ring = [(i, j) for i in (up, lon, down) for j in (west, lat, east)]
     del ring[4]
     for device in ring + steps:
         pl.semaphore_signal(barrier, inc=1, device_id=device, device_id_type=MESH)
 
+    for i in range(lon_t):
+        stage[i * lat_t : (i + 1) * lat_t] = coarse_in[i].astype(F32)
+    tok[0:own] = stage[...].astype(BF16)
     zero = jnp.zeros((3, ch, ch), BF16)
     for conv in range(2):
         w[conv, 3, :, :, pl.ds(0, ch)] = zero
@@ -163,7 +164,6 @@
                 step_copy(s + 1).start()
             state["at"] = s + 1
 
-    local[0].wait()
     step_copy(0).start()
 
     def remote(src, dst, at, device):
@@ -181,7 +181,7 @@
     to_down.start()
     to_up.start()
 
-    local[1].wait()
+    local[0].wait()
     cols_s[0] = fine[:, :, 0:16, :].astype(F32)[:, :, 0:1, :]
     cols_s[1] = fine[:, :, width - 16 : width, :].astype(F32)[:, :, 15:16, :]
     side_copies = []
@@ -217,21 +217,44 @@
     gain1 = norm_gains[1:2, :]
     n0 = chunk_of(pairs, 4)
 
+    def put(dst, at, n, q, v, slot):
+        base = q * 3 * ch
+        room = hb.at[slot]
+        room[0:n, q, LEFT : LEFT + width, :] = v
+        dst[pl.ds(at, n), :, base + ch : base + 2 * ch] = v.astype(BF16)
+        for b in (0, 2):
+            lo = LEFT - 1 + b
+            col = base + b * ch
+            dst[pl.ds(at, n), :, col : col + ch] = room[0:n, q, lo : lo + width, :].astype(BF16)
+
+    def patch(dst, cols):
+        row = lax.broadcasted_iota(jnp.int32, (1, 16, ch), 1)
+        for q in range(2):
+            for side, lo, at in ((0, 0, 0), (1, width - 16, 15)):
+                col = (q * 3 + 2 * side) * ch
+                old = dst[:, lo : lo + 16, col : col + ch].astype(F32)
+                new = jnp.where(row == at, cols[side][:, q], old)
+                dst[:, lo : lo + 16, col : col + ch] = new.astype(BF16)
+
     def first(i, c):
         at = pl.multiple_of(i * n0, n0)
-        v = fine[pl.ds(at, n0)].astype(F32)
-        h1[pl.ds(at + 1, n0), :, LEFT : LEFT + width, :] = norm_silu(v, ones, gain0)
+        v = norm_silu(fine[pl.ds(at, n0)].astype(F32), ones, gain0)
+        for q in range(2):
+            put(x1, at + 1, n0, q, v[:, q], q)
         return c
 
-    lax.fori_loop(0, pairs // n0, first, 0)
+    loops = pairs // n0
+    lax.fori_loop(0, loops // 2, first, 0)
+    advance()
+    lax.fori_loop(loops // 2, loops, first, 0)
     advance()
 
     to_down.wait()
     to_up.wait()
-    v = halo[...].astype(F32)
-    v = norm_silu(v, ones, gain0)
-    h1[0:1, :, LEFT : LEFT + width, :] = v[0:1]
-    h1[pairs + 1 : pairs + 2, :, LEFT : LEFT + width, :] = v[1:2]
+    v = norm_silu(halo[...].astype(F32), ones, gain0)
+    for q in range(2):
+        put(x1, 0, 1, q, v[0:1, q], 0)
+        put(x1, pairs + 1, 1, q, v[1:2, q], 1)
 
     def wait_send(side):
         for copy in side_copies[side]:
@@ -246,61 +269,46 @@
     pl.when(has_east)(lambda: wait_recv(0))
     pl.when(has_west)(lambda: wait_recv(1))
     gain0c = gain0.reshape(1, 1, 1, ch)
-    for side, at in ((0, LEFT - 1), (1, LEFT + width)):
+    sides = []
+    for side in range(2):
         v = cols_r[side]
         ms = jnp.mean(v * v, axis=-1, keepdims=True)
-        h1[:, :, at : at + 1, :] = silu(v * lax.rsqrt(ms + 1e-6) * gain0c)
-
-    def pack(src, count):
-        n = chunk_of(count, 3)
-
-        def go(i, c):
-            at = i * n
-            for q in range(2):
-                for b in range(3):
-                    lo = LEFT - 1 + b
-                    col = (q * 3 + b) * ch
-                    x[pl.ds(at, n), :, col : col + ch] = src[
-                        pl.ds(at, n), q, lo : lo + width, :
-                    ].astype(BF16)
-            return c
-
-        lax.fori_loop(0, count // n, go, 0)
-
-    pack(h1, pairs + 2)
+        sides.append(silu(v * lax.rsqrt(ms + 1e-6) * gain0c))
+    patch(x1, sides)
     advance()
     for copy in taps:
         copy.wait()
 
     half_k = 6 * ch
 
-    def conv(at, n, conv_at):
+    def conv(x, at, n, conv_at):
         wa = w[conv_at, 0:2].reshape(half_k, 2 * ch)
         wb = w[conv_at, 2:4].reshape(half_k, 2 * ch)
         a = x[pl.ds(at, n)].reshape(n * width, half_k)
         b = x[pl.ds(at + 1, n)].reshape(n * width, half_k)
         return mm(a, wa) + mm(b, wb)
 
-    n1 = chunk_of(pairs + 1, 5)
+    n1 = chunk_of(pairs + 1, 13)
 
     def second(i, c):
         at = i * n1
-        y = conv(at, n1, 0)
-        ms = mm((y * y).astype(BF16), ones2)
-        z = y * lax.rsqrt(ms + 1e-6)
-        for q in range(2):
-            v = silu(z[:, q * ch : (q + 1) * ch] * gain1)
-            h2[pl.ds(at, n1), q, LEFT : LEFT + width, :] = v.reshape(n1, width, ch)
+        parts = ((0, (n1 + 1) // 2), ((n1 + 1) // 2, n1))
+        results = [conv(x1, at + lo, hi - lo, 0) for lo, hi in parts]
+        for slot, (lo, hi) in enumerate(parts):
+            y, n = results[slot], hi - lo
+            ms = mm((y * y).astype(BF16), ones2)
+            z = y * lax.rsqrt(ms + 1e-6)
+            for q in range(2):
+                v = silu(z[:, q * ch : (q + 1) * ch] * gain1).reshape(n, width, ch)
+                put(x2, at + lo, n, q, v, slot)
+                cols2_s[0, pl.ds(at + lo, n), q] = v[:, 0:1]
+                cols2_s[1, pl.ds(at + lo, n), q] = v[:, width - 1 : width]
         return c
 
     loops = (pairs + 1) // n1
-    lax.fori_loop(0, loops // 2, second, 0)
+    lax.fori_loop(0, (loops + 1) // 2, second, 0)
     advance()
-    lax.fori_loop(loops // 2, loops, second, 0)
-    advance()
-
-    cols2_s[0] = h2[:, :, LEFT : LEFT + 1, :]
-    cols2_s[1] = h2[:, :, LEFT + width - 1 : LEFT + width, :]
+    lax.fori_loop((loops + 1) // 2, loops, second, 0)
 
     def remote2(side, there):
         return pltpu.make_async_remote_copy(
@@ -316,7 +324,7 @@
     pl.when(has_west)(to_west.start)
     pl.when(has_east)(to_east.start)
 
-    for copy in local[2:]:
+    for copy in local[1:]:
         copy.wait()
     heads = wide // head_gains.shape[1]
     hd = wide // heads
@@ -331,16 +339,13 @@
     def norm_heads(v, g):
         return v * lax.rsqrt(mm((v * v).astype(BF16), per_head) + 1e-6) * g
 
-    mine = tok[0:own].astype(F32)
+    mine = stage[...]
     q = norm_heads(mm(norm_tokens(mine), wq[...]), gq) * (1.0 / math.sqrt(hd))
     r = lax.broadcasted_iota(jnp.int32, (heads * own, wide), 0) // own
     c = lax.broadcasted_iota(jnp.int32, (heads * own, wide), 1) // hd
     head_mask = r == c
     qb = jnp.where(head_mask, jnp.concatenate([q] * heads, axis=0), 0.0).astype(BF16)
-    while state["at"] < len(steps):
-        advance()
-    total = own * lon_n * lat_n
-    nt = min(256, total)
+    nt = 8 * own
 
     def attend(i, carry):
         acc, tot = carry
@@ -352,18 +357,21 @@
         e = jnp.exp(s)
         return acc + mm(e.astype(BF16), vv), tot + jnp.sum(e, axis=1, keepdims=True)
 
-    acc, tot = lax.fori_loop(
-        0,
-        total // nt,
-        attend,
-        (jnp.zeros((heads * own, wide), F32), jnp.zeros((heads * own, 1), F32)),
-    )
+    carry = (jnp.zeros((heads * own, wide), F32), jnp.zeros((heads * own, 1), F32))
+    done = 0
+    while done < lon_n * lat_n // 8:
+        ready = (1 << state["at"]) // 8
+        if ready > done:
+            carry = lax.fori_loop(done, ready, attend, carry)
+            done = ready
+        advance()
+    acc, tot = carry
     att = jnp.where(head_mask, acc / tot, 0.0).reshape(heads, own, wide)
     att = jnp.sum(att, axis=0).astype(BF16)
     coarse = (mine + mm(att, wo[...])).astype(BF16)
-    coarse_out[...] = coarse
-    lon_t = lift.shape[0]
-    lat_t = own // lon_t
+    stage[...] = coarse.astype(F32)
+    for i in range(lon_t):
+        coarse_out[i] = stage[i * lat_t : (i + 1) * lat_t].astype(BF16)
     rr = lax.broadcasted_iota(jnp.int32, (lon_t * width, own), 0) // (width // lat_t)
     cc = lax.broadcasted_iota(jnp.int32, (lon_t * width, own), 1)
     rep = mm(jnp.where(rr == cc, 1.0, 0.0).astype(BF16), coarse).astype(BF16)
@@ -373,9 +381,7 @@
     pl.when(has_east)(to_east.wait_send)
     pl.when(has_east)(to_west.wait_recv)
     pl.when(has_west)(to_east.wait_recv)
-    h2[:, :, LEFT - 1 : LEFT, :] = cols2_r[0]
-    h2[:, :, LEFT + width : LEFT + width + 1, :] = cols2_r[1]
-    pack(h2, pairs + 1)
+    patch(x2, cols2_r)
     n2 = pairs // lon_t
 
     def out_copy(i):
@@ -385,18 +391,20 @@
         )
 
     def third(i, c):
-        at = pl.multiple_of(i * n2, n2)
-        y = conv(at, n2, 1)
-        up_row = lift[i]
-        for q in range(2):
-            v = y[:, q * ch : (q + 1) * ch].reshape(n2, width, ch)
-            outs[pl.ds(at, n2), q] = (
-                fine[pl.ds(at, n2), q].astype(F32) + v + up_row[None]
-            ).astype(BF16)
-        out_copy(i).start()
+        results = [conv(x2, pl.multiple_of((2 * i + k) * n2, n2), n2, 1) for k in range(2)]
+        for k in range(2):
+            at = pl.multiple_of((2 * i + k) * n2, n2)
+            y = results[k]
+            up_row = lift[2 * i + k]
+            for q in range(2):
+                v = y[:, q * ch : (q + 1) * ch].reshape(n2, width, ch)
+                outs[pl.ds(at, n2), q] = (
+                    fine[pl.ds(at, n2), q].astype(F32) + v + up_row[None]
+                ).astype(BF16)
+            out_copy(2 * i + k).start()
         return c
 
-    lax.fori_loop(0, lon_t, third, 0)
+    lax.fori_loop(0, lon_t // 2, third, 0)
     for i in range(lon_t):
         out_copy(i).wait()
 
@@ -413,15 +421,16 @@
         functools.partial(body, lon_n, lat_n),
         out_shape=(
             jax.ShapeDtypeStruct((pairs, 2, width, ch), BF16),
-            jax.ShapeDtypeStruct((own, wide), BF16),
+            jax.ShapeDtypeStruct(coarse_state.shape, BF16),
         ),
-        in_specs=[any_, any_, vm, any_, vm, vm, any_, any_, any_, any_],
+        in_specs=[any_, vm, vm, any_, vm, vm, any_, any_, any_, any_],
         out_specs=(any_, vm),
         scratch_shapes=[
             pltpu.VMEM((pairs, 2, width, ch), BF16),
-            pltpu.VMEM((pairs + 2, 2, width + 16, ch), F32),
-            pltpu.VMEM((pairs + 1, 2, width + 16, ch), F32),
+            pltpu.VMEM((2, 7, 2, width + 16, ch), F32),
             pltpu.VMEM((pairs + 2, width, 6 * ch), BF16),
+            pltpu.VMEM((pairs + 1, width, 6 * ch), BF16),
+            pltpu.VMEM((own, wide), F32),
             pltpu.VMEM((2, 4, 3, ch, 2 * ch), BF16),
             pltpu.VMEM(query_weight.shape, BF16),
             pltpu.VMEM(keyvalue_weight.shape, BF16),
@@ -435,7 +444,7 @@
             pltpu.VMEM((2, pairs + 2, 2, 1, ch), F32),
             pltpu.VMEM((2, pairs + 1, 2, 1, ch), F32),
             pltpu.VMEM((2, pairs + 1, 2, 1, ch), F32),
-            sem((6,)),
+            sem((5,)),
             sem((12,)),
             sem((lon_t,)),
             sem((8,)),
@@ -450,7 +459,7 @@
         ),
     )(
         fine_state.reshape(pairs, 2, width, ch),
-        coarse_state.reshape(own, wide),
+        coarse_state,
         norm_gains,
         kernels,
         token_gain.reshape(1, wide),
@@ -460,7 +469,7 @@
         output_weight,
         expand_weight,
     )
-    return fine_result.reshape(fine_state.shape), coarse_result.reshape(coarse_state.shape)
+    return fine_result.reshape(fine_state.shape), coarse_result
 
 
 def solution(mesh):

time: 45.9 us -> 42.3 us (0.922)
  local copies, waits for them, and re-layouts: 5.85 us -> 3.7 us
  Pallas kernels: 39.1 us -> 37.7 us
    reshape x2 -> x0, local copies, waits for them, and re-layouts: 2.77 us -> none  [the longest x1 1.39 us: local(): coarse_result.reshape(coarse_state.shape)]
    pallas_call x1, Pallas kernels: 39.1 us -> 37.7 us  [local(): pl.pallas_call(functools.partial(body, lon_n, lat_n), out_shape=(jax.Shap...]
    unnamed x1 -> x4, local copies, waits for them, and re-layouts: 3.08 us -> 3.7 us
where the time goes in v3:
time: 42.3 us; the launch traced here: 42.1 us
  Pallas kernels  37.7 us (89%)
  local copies, waits for them, and re-layouts  3.7 us (9%)
  between operations  0.65 us (2%)
    pallas_call x1, Pallas kernels, local(): pl.pallas_call(functools.partial(body, lon_n, lat_n), out_shape=(jax.Shap...  37.7 us
    unnamed x4, local copies, waits for them, and re-layouts  3.7 us

profile of v3, /device:TPU:0, one launch (start us, length us, event | category | flops | bytes accessed | tf_op | source)
XLA Modules:
  0.0 42.1 jit_solution(15217941055629486865)
XLA Ops:
  0.6 37.7 %shard_map.113 = (bf16[64,2,64,128]{3,2,1,0:T(8,128)(2,1)}, bf16[8,4,512]{2,1,0:T(4,128)(2,1)}) custom-call(bf16[64,2,64,128]{3,2,1,0:T(8,128)(2,1)} %bitcast.3, bf16[8,4,512]{2,1,0:T(4,128)(2,1)} %coarse_in.1, f32[2,128]{1,0:T(2,128)} %norm_gains.1, bf16[2,3,3,128,128]{4,3,2,1,0:T(8,128)(2,1)} %kernels_hbm.1, f32[1,512]{1,0:T(1,128)} %bitcast.5, ...), custom_call_target="tpu_custom_call" | custom-call | tf_op jit(solution)/shard_map/pallas_call | solution.py:420
  38.4 0.0 copy-start
  38.4 3.1 %copy.14 = bf16[128,64,128]{2,1,0:T(8,128)(2,1)} copy(bf16[128,64,128]{2,1,0:T(8,128)(2,1)} %bitcast.4) | data formatting | bytes 4194304
  41.5 0.0 copy-done
  41.5 0.6 %copy.15 = bf16[8,4,512]{2,1,0:T(4,128)(2,1)} copy(bf16[8,4,512]{2,1,0:T(4,128)(2,1)S(1)} %copy-done) | data formatting | bytes 65536
Async XLA Ops:
  38.4 3.1 %copy-start = (bf16[8,4,512]{2,1,0:T(4,128)(2,1)S(1)}, bf16[8,4,512]{2,1,0:T(4,128)(2,1)}, u32[]{:S(2)}) copy-start(bf16[8,4,512]{2,1,0:T(4,128)(2,1)} %get-tuple-element.9) | copy-start | bytes 98308

commit v4 on v3

--- a/solution.py
+++ b/solution.py
@@ -42,39 +42,31 @@
 def body(
     lon_n,
     lat_n,
-    fine_hbm,
+    fine,
     coarse_in,
     norm_gains,
-    kernels_hbm,
+    kernels,
     token_gain,
     head_gains,
-    wq_hbm,
-    wkv_hbm,
-    wo_hbm,
-    we_hbm,
-    out_hbm,
+    wq,
+    wkv,
+    wo,
+    we,
+    outs,
     coarse_out,
-    fine,
     hb,
     x1,
     x2,
     stage,
     w,
-    wq,
-    wkv,
-    wo,
-    we,
     tok,
     lift,
-    outs,
     halo,
     cols_s,
     cols_r,
     cols2_s,
     cols2_r,
-    dma,
     wsem,
-    osem,
     hs,
     hr,
     c2s,
@@ -91,35 +83,33 @@
     west, east = lax.rem(lat + lat_n - 1, lat_n), lax.rem(lat + 1, lat_n)
     has_west, has_east = lat > 0, lat < lat_n - 1
 
-    steps = []
-    d = lat_n // 2
-    while d:
-        steps.append((lon, lat + d - 2 * d * ((lat // d) % 2)))
-        d //= 2
-    d = lon_n // 2
-    while d:
-        steps.append((lon + d - 2 * d * ((lon // d) % 2), lat))
-        d //= 2
-
-    local = [
-        pltpu.make_async_copy(fine_hbm, fine, dma.at[0]),
-        pltpu.make_async_copy(wq_hbm, wq, dma.at[1]),
-        pltpu.make_async_copy(wkv_hbm, wkv, dma.at[2]),
-        pltpu.make_async_copy(wo_hbm, wo, dma.at[3]),
-        pltpu.make_async_copy(we_hbm, we, dma.at[4]),
-    ]
+    by_z = ("lat", 2, lat_n // 2)
+    by_x = ("lat", 1, 2)
+    by_y = ("lon", 2, lon_n // 2)
+    by_core = ("lon", 1, 2)
+    chains = ((by_z, by_x, by_y, by_core), (by_z, by_y, by_x, by_core))
+
+    def member(stage_at, offset):
+        axis, stride, group = stage_at
+        index = lon if axis == "lon" else lat
+        place = (index // stride) % group
+        moved = index + ((place + offset) % group - place) * stride
+        return (moved, lat) if axis == "lon" else (lon, moved)
+
+    partners = [member(stage_at, o) for stage_at in chains[0] for o in range(1, stage_at[2])]
+
     taps = []
     for conv in range(2):
         for r in range(2):
             for a in range(3):
                 taps.append(
                     pltpu.make_async_copy(
-                        kernels_hbm.at[conv, a],
+                        kernels.at[conv, a],
                         w.at[conv, a + r, :, :, pl.ds(r * ch, ch)],
                         wsem.at[len(taps)],
                     )
                 )
-    for copy in local[:1] + taps + local[1:]:
+    for copy in taps:
         copy.start()
 
     cols_r[...] = jnp.zeros_like(cols_r)
@@ -128,12 +118,14 @@
     barrier = pltpu.get_barrier_semaphore()
     ring = [(i, j) for i in (up, lon, down) for j in (west, lat, east)]
     del ring[4]
-    for device in ring + steps:
+    for device in ring + partners:
         pl.semaphore_signal(barrier, inc=1, device_id=device, device_id_type=MESH)
 
     for i in range(lon_t):
         stage[i * lat_t : (i + 1) * lat_t] = coarse_in[i].astype(F32)
-    tok[0:own] = stage[...].astype(BF16)
+    half_own = own // 2
+    for half in range(2):
+        tok[half, 0:half_own] = stage[half * half_own : (half + 1) * half_own].astype(BF16)
     zero = jnp.zeros((3, ch, ch), BF16)
     for conv in range(2):
         w[conv, 3, :, :, pl.ds(0, ch)] = zero
@@ -141,30 +133,47 @@
     ones = block_ones(ch, ch, 1.0 / ch)
     ones2 = block_ones(2 * ch, ch, 1.0 / ch)
 
-    pl.semaphore_wait(barrier, len(ring) + len(steps))
-
-    def step_copy(s):
-        size = own << s
-        return pltpu.make_async_remote_copy(
-            src_ref=tok.at[pl.ds(0, size)],
-            dst_ref=tok.at[pl.ds(size, size)],
-            send_sem=ts.at[s],
-            recv_sem=tr.at[s],
-            device_id=steps[s],
-            device_id_type=MESH,
-        )
+    pl.semaphore_wait(barrier, len(ring) + len(partners))
+
+    def stage_copies(level):
+        copies = []
+        for half in range(2):
+            size, base = half_own, 0
+            for done_stage in chains[half][:level]:
+                size *= done_stage[2]
+                base += done_stage[2] - 1
+            for o in range(1, chains[half][level][2]):
+                copies.append(
+                    pltpu.make_async_remote_copy(
+                        src_ref=tok.at[half, pl.ds(0, size)],
+                        dst_ref=tok.at[half, pl.ds(o * size, size)],
+                        send_sem=ts.at[half, base + o - 1],
+                        recv_sem=tr.at[half, base + o - 1],
+                        device_id=member(chains[half][level], o),
+                        device_id_type=MESH,
+                    )
+                )
+        return copies
+
+    def held(level):
+        return [half_own * math.prod(g[2] for g in chain[:level]) for chain in chains]
 
     state = {"at": 0}
 
+    def start_stage(level):
+        for copy in stage_copies(level):
+            copy.start()
+
     def advance():
-        s = state["at"]
-        if s < len(steps):
-            step_copy(s).wait()
-            if s + 1 < len(steps):
-                step_copy(s + 1).start()
-            state["at"] = s + 1
-
-    step_copy(0).start()
+        level = state["at"]
+        if level < 4:
+            for copy in stage_copies(level):
+                copy.wait()
+            if level < 3:
+                start_stage(level + 1)
+            state["at"] = level + 1
+
+    start_stage(0)
 
     def remote(src, dst, at, device):
         return pltpu.make_async_remote_copy(
@@ -176,12 +185,11 @@
             device_id_type=MESH,
         )
 
-    to_down = remote(fine_hbm.at[pl.ds(pairs - 1, 1)], halo.at[pl.ds(0, 1)], 0, (down, lat))
-    to_up = remote(fine_hbm.at[pl.ds(0, 1)], halo.at[pl.ds(1, 1)], 1, (up, lat))
+    to_down = remote(fine.at[pl.ds(pairs - 1, 1)], halo.at[pl.ds(0, 1)], 0, (down, lat))
+    to_up = remote(fine.at[pl.ds(0, 1)], halo.at[pl.ds(1, 1)], 1, (up, lat))
     to_down.start()
     to_up.start()
 
-    local[0].wait()
     cols_s[0] = fine[:, :, 0:16, :].astype(F32)[:, :, 0:1, :]
     cols_s[1] = fine[:, :, width - 16 : width, :].astype(F32)[:, :, 15:16, :]
     side_copies = []
@@ -243,11 +251,7 @@
             put(x1, at + 1, n0, q, v[:, q], q)
         return c
 
-    loops = pairs // n0
-    lax.fori_loop(0, loops // 2, first, 0)
-    advance()
-    lax.fori_loop(loops // 2, loops, first, 0)
-    advance()
+    lax.fori_loop(0, pairs // n0, first, 0)
 
     to_down.wait()
     to_up.wait()
@@ -324,8 +328,6 @@
     pl.when(has_west)(to_west.start)
     pl.when(has_east)(to_east.start)
 
-    for copy in local[1:]:
-        copy.wait()
     heads = wide // head_gains.shape[1]
     hd = wide // heads
     tg = token_gain[...]
@@ -345,11 +347,10 @@
     c = lax.broadcasted_iota(jnp.int32, (heads * own, wide), 1) // hd
     head_mask = r == c
     qb = jnp.where(head_mask, jnp.concatenate([q] * heads, axis=0), 0.0).astype(BF16)
-    nt = 8 * own
-
-    def attend(i, carry):
+
+    def attend(half, nt, i, carry):
         acc, tot = carry
-        t = tok[pl.ds(pl.multiple_of(i * nt, nt), nt)].astype(F32)
+        t = tok[half, pl.ds(pl.multiple_of(i * nt, nt), nt)].astype(F32)
         kv = mm(norm_tokens(t), wkv[...])
         k = norm_heads(kv[:, :wide], gk).astype(BF16)
         vv = kv[:, wide:].astype(BF16)
@@ -358,12 +359,18 @@
         return acc + mm(e.astype(BF16), vv), tot + jnp.sum(e, axis=1, keepdims=True)
 
     carry = (jnp.zeros((heads * own, wide), F32), jnp.zeros((heads * own, 1), F32))
-    done = 0
-    while done < lon_n * lat_n // 8:
-        ready = (1 << state["at"]) // 8
-        if ready > done:
-            carry = lax.fori_loop(done, ready, attend, carry)
-            done = ready
+    done = [0, 0]
+    while True:
+        for half, ready in enumerate(held(state["at"])):
+            more = ready - done[half]
+            if more >= 128:
+                nt = 256 if more % 256 == 0 and done[half] % 256 == 0 else 128
+                carry = lax.fori_loop(
+                    done[half] // nt, ready // nt, functools.partial(attend, half, nt), carry
+                )
+                done[half] = ready
+        if state["at"] == 4:
+            break
         advance()
     acc, tot = carry
     att = jnp.where(head_mask, acc / tot, 0.0).reshape(heads, own, wide)
@@ -384,12 +391,6 @@
     patch(x2, cols2_r)
     n2 = pairs // lon_t
 
-    def out_copy(i):
-        at = pl.multiple_of(i * n2, n2)
-        return pltpu.make_async_copy(
-            outs.at[pl.ds(at, n2)], out_hbm.at[pl.ds(at, n2)], osem.at[i]
-        )
-
     def third(i, c):
         results = [conv(x2, pl.multiple_of((2 * i + k) * n2, n2), n2, 1) for k in range(2)]
         for k in range(2):
@@ -401,12 +402,9 @@
                 outs[pl.ds(at, n2), q] = (
                     fine[pl.ds(at, n2), q].astype(F32) + v + up_row[None]
                 ).astype(BF16)
-            out_copy(2 * i + k).start()
         return c
 
     lax.fori_loop(0, lon_t // 2, third, 0)
-    for i in range(lon_t):
-        out_copy(i).wait()
 
 
 def local(lon_n, lat_n, fine_state, coarse_state, norm_gains, kernels, token_gain, head_gains,
@@ -414,8 +412,9 @@
     rows, width, ch = fine_state.shape
     lon_t, lat_t, wide = coarse_state.shape
     pairs, own = rows // 2, lon_t * lat_t
-    hops = int(math.log2(lon_n)) + int(math.log2(lat_n))
-    any_, vm = pl.BlockSpec(memory_space=pl.ANY), pl.BlockSpec(memory_space=pltpu.VMEM)
+    hops = lat_n // 2 + lon_n // 2
+    tokens = own * lon_n * lat_n
+    vm = pl.BlockSpec(memory_space=pltpu.VMEM)
     sem = pltpu.SemaphoreType.DMA
     fine_result, coarse_result = pl.pallas_call(
         functools.partial(body, lon_n, lat_n),
@@ -423,39 +422,31 @@
             jax.ShapeDtypeStruct((pairs, 2, width, ch), BF16),
             jax.ShapeDtypeStruct(coarse_state.shape, BF16),
         ),
-        in_specs=[any_, vm, vm, any_, vm, vm, any_, any_, any_, any_],
-        out_specs=(any_, vm),
+        in_specs=[vm] * 10,
+        out_specs=(vm, vm),
         scratch_shapes=[
-            pltpu.VMEM((pairs, 2, width, ch), BF16),
             pltpu.VMEM((2, 7, 2, width + 16, ch), F32),
             pltpu.VMEM((pairs + 2, width, 6 * ch), BF16),
             pltpu.VMEM((pairs + 1, width, 6 * ch), BF16),
             pltpu.VMEM((own, wide), F32),
             pltpu.VMEM((2, 4, 3, ch, 2 * ch), BF16),
-            pltpu.VMEM(query_weight.shape, BF16),
-            pltpu.VMEM(keyvalue_weight.shape, BF16),
-            pltpu.VMEM(output_weight.shape, BF16),
-            pltpu.VMEM(expand_weight.shape, BF16),
-            pltpu.VMEM((own * lon_n * lat_n, wide), BF16),
+            pltpu.VMEM((2, tokens // 2, wide), BF16),
             pltpu.VMEM((lon_t, width, ch), F32),
-            pltpu.VMEM((pairs, 2, width, ch), BF16),
             pltpu.VMEM((2, 2, width, ch), BF16),
             pltpu.VMEM((2, pairs, 2, 1, ch), F32),
             pltpu.VMEM((2, pairs + 2, 2, 1, ch), F32),
             pltpu.VMEM((2, pairs + 1, 2, 1, ch), F32),
             pltpu.VMEM((2, pairs + 1, 2, 1, ch), F32),
-            sem((5,)),
             sem((12,)),
-            sem((lon_t,)),
             sem((8,)),
             sem((8,)),
             sem((2,)),
             sem((2,)),
-            sem((hops,)),
-            sem((hops,)),
+            sem((2, hops)),
+            sem((2, hops)),
         ],
         compiler_params=pltpu.CompilerParams(
-            collective_id=0, has_side_effects=True, vmem_limit_bytes=56 * 2**20
+            collective_id=0, has_side_effects=True, vmem_limit_bytes=36 * 2**20 + 2 * tokens * wide
         ),
     )(
         fine_state.reshape(pairs, 2, width, ch),

time: 42.3 us -> 43.7 us (1.033)
  the two profiles are of different devices: /device:TPU:0 before, /device:TPU:3 now
where the time goes in v4:
time: 43.7 us; the launch traced here: 43.2 us
  Pallas kernels  31 us (71%)
  local copies, waits for them, and re-layouts  11.6 us (27%)
  between operations  0.66 us (2%)
    pallas_call x1, Pallas kernels, local(): pl.pallas_call(functools.partial(body, lon_n, lat_n), out_shape=(jax.Shap...  31 us
    unnamed x22, local copies, waits for them, and re-layouts  11.6 us

profile of v4, /device:TPU:3, one launch (start us, length us, event | category | flops | bytes accessed | tf_op | source)
XLA Modules:
  0.0 43.2 jit_solution(4106549621807734426)
XLA Ops:
  0.6 0.0 copy-start
  0.6 1.6 %copy-done = bf16[128,64,128]{2,1,0:T(8,128)(2,1)S(1)} copy-done((bf16[128,64,128]{2,1,0:T(8,128)(2,1)S(1)}, bf16[128,64,128]{2,1,0:T(8,128)(2,1)}, u32[]{:S(2)}) %copy-start) | copy-done | bytes 2097176
  2.2 0.0 copy-start.1
  2.2 1.2 %copy-done.1 = bf16[512,1024]{1,0:T(8,128)(2,1)S(1)} copy-done((bf16[512,1024]{1,0:T(8,128)(2,1)S(1)}, bf16[512,1024]{1,0:T(8,128)(2,1)}, u32[]{:S(2)}) %copy-start.1) | copy-done | bytes 1048600
  3.5 0.0 copy-start.2
  3.5 1.1 %copy-done.2 = bf16[2,3,3,128,128]{4,3,2,1,0:T(8,128)(2,1)S(1)} copy-done((bf16[2,3,3,128,128]{4,3,2,1,0:T(8,128)(2,1)S(1)}, bf16[2,3,3,128,128]{4,3,2,1,0:T(8,128)(2,1)}, u32[]{:S(2)}) %copy-start.2) | copy-done | bytes 589848
  4.5 0.0 copy-start.3
  4.5 1.0 %copy-done.3 = bf16[512,512]{1,0:T(8,128)(2,1)S(1)} copy-done((bf16[512,512]{1,0:T(8,128)(2,1)S(1)}, bf16[512,512]{1,0:T(8,128)(2,1)}, u32[]{:S(2)}) %copy-start.3) | copy-done | bytes 524312
  5.6 0.0 copy-start.4
  5.6 1.0 %copy-done.4 = bf16[512,512]{1,0:T(8,128)(2,1)S(1)} copy-done((bf16[512,512]{1,0:T(8,128)(2,1)S(1)}, bf16[512,512]{1,0:T(8,128)(2,1)}, u32[]{:S(2)}) %copy-start.4) | copy-done | bytes 524312
  6.6 0.0 copy-start.5
  6.6 0.9 %copy-done.5 = bf16[512,128]{1,0:T(8,128)(2,1)S(1)} copy-done((bf16[512,128]{1,0:T(8,128)(2,1)S(1)}, bf16[512,128]{1,0:T(8,128)(2,1)}, u32[]{:S(2)}) %copy-start.5) | copy-done | bytes 131096
  7.5 0.0 copy-start.6
  7.5 0.8 %copy-done.6 = bf16[8,4,512]{2,1,0:T(4,128)(2,1)S(1)} copy-done((bf16[8,4,512]{2,1,0:T(4,128)(2,1)S(1)}, bf16[8,4,512]{2,1,0:T(4,128)(2,1)}, u32[]{:S(2)}) %copy-start.6) | copy-done | bytes 32792
  8.3 0.0 copy-start.7
  8.3 0.7 %copy-done.7 = f32[512]{0:T(512)S(1)} copy-done((f32[512]{0:T(512)S(1)}, f32[512]{0:T(512)}, u32[]{:S(2)}) %copy-start.7) | copy-done | bytes 2072
  8.9 0.0 copy-start.8
  8.9 0.7 %copy-done.8 = f32[2,128]{1,0:T(2,128)S(1)} copy-done((f32[2,128]{1,0:T(2,128)S(1)}, f32[2,128]{1,0:T(2,128)}, u32[]{:S(2)}) %copy-start.8) | copy-done | bytes 1048
  9.6 0.0 copy-start.9
  9.6 0.7 %copy-done.9 = f32[2,64]{1,0:T(2,128)S(1)} copy-done((f32[2,64]{1,0:T(2,128)S(1)}, f32[2,64]{1,0:T(2,128)}, u32[]{:S(2)}) %copy-start.9) | copy-done | bytes 536
  10.3 31.0 %shard_map.113 = (bf16[64,2,64,128]{3,2,1,0:T(8,128)(2,1)S(1)}, bf16[8,4,512]{2,1,0:T(4,128)(2,1)S(1)}) custom-call(bf16[64,2,64,128]{3,2,1,0:T(8,128)(2,1)S(1)} %bitcast.3, bf16[8,4,512]{2,1,0:T(4,128)(2,1)S(1)} %copy-done.6, f32[2,128]{1,0:T(2,128)S(1)} %copy-done.8, bf16[2,3,3,128,128]{4,3,2,1,0:T(8,128)(2,1)S(1)} %copy-done.2, f32[1,512]{1,0:T(1,128)S(1)} %bitcast.5, ...), custom_call_target="tpu_custom_call" | custom-call | tf_op jit(solution)/shard_map/pallas_call | solution.py:419
  41.3 1.3 %copy.14 = bf16[128,64,128]{2,1,0:T(8,128)(2,1)} copy(bf16[128,64,128]{2,1,0:T(8,128)(2,1)S(1)} %bitcast.4) | data formatting | bytes 4194304
  42.6 0.6 %copy.15 = bf16[8,4,512]{2,1,0:T(4,128)(2,1)} copy(bf16[8,4,512]{2,1,0:T(4,128)(2,1)S(1)} %get-tuple-element.9) | data formatting | bytes 65536
Async XLA Ops:
  0.6 1.6 %copy-start = (bf16[128,64,128]{2,1,0:T(8,128)(2,1)S(1)}, bf16[128,64,128]{2,1,0:T(8,128)(2,1)}, u32[]{:S(2)}) copy-start(bf16[128,64,128]{2,1,0:T(8,128)(2,1)} %param.10) | copy-start | bytes 6291460
  2.2 1.2 %copy-start.1 = (bf16[512,1024]{1,0:T(8,128)(2,1)S(1)}, bf16[512,1024]{1,0:T(8,128)(2,1)}, u32[]{:S(2)}) copy-start(bf16[512,1024]{1,0:T(8,128)(2,1)} %wkv.1) | copy-start | bytes 3145732
  3.5 1.1 %copy-start.2 = (bf16[2,3,3,128,128]{4,3,2,1,0:T(8,128)(2,1)S(1)}, bf16[2,3,3,128,128]{4,3,2,1,0:T(8,128)(2,1)}, u32[]{:S(2)}) copy-start(bf16[2,3,3,128,128]{4,3,2,1,0:T(8,128)(2,1)} %kernels.1) | copy-start | bytes 1769476
  4.5 1.0 %copy-start.3 = (bf16[512,512]{1,0:T(8,128)(2,1)S(1)}, bf16[512,512]{1,0:T(8,128)(2,1)}, u32[]{:S(2)}) copy-start(bf16[512,512]{1,0:T(8,128)(2,1)} %wq.1) | copy-start | bytes 1572868
  5.6 1.0 %copy-start.4 = (bf16[512,512]{1,0:T(8,128)(2,1)S(1)}, bf16[512,512]{1,0:T(8,128)(2,1)}, u32[]{:S(2)}) copy-start(bf16[512,512]{1,0:T(8,128)(2,1)} %wo.1) | copy-start | bytes 1572868
  6.6 0.9 %copy-start.5 = (bf16[512,128]{1,0:T(8,128)(2,1)S(1)}, bf16[512,128]{1,0:T(8,128)(2,1)}, u32[]{:S(2)}) copy-start(bf16[512,128]{1,0:T(8,128)(2,1)} %we.1) | copy-start | bytes 393220
  7.5 0.8 %copy-start.6 = (bf16[8,4,512]{2,1,0:T(4,128)(2,1)S(1)}, bf16[8,4,512]{2,1,0:T(4,128)(2,1)}, u32[]{:S(2)}) copy-start(bf16[8,4,512]{2,1,0:T(4,128)(2,1)} %coarse_in.1) | copy-start | bytes 98308
  8.3 0.7 %copy-start.7 = (f32[512]{0:T(512)S(1)}, f32[512]{0:T(512)}, u32[]{:S(2)}) copy-start(f32[512]{0:T(512)} %param.14) | copy-start | bytes 6148
  8.9 0.7 %copy-start.8 = (f32[2,128]{1,0:T(2,128)S(1)}, f32[2,128]{1,0:T(2,128)}, u32[]{:S(2)}) copy-start(f32[2,128]{1,0:T(2,128)} %norm_gains.1) | copy-start | bytes 3076
  9.6 0.7 %copy-start.9 = (f32[2,64]{1,0:T(2,128)S(1)}, f32[2,64]{1,0:T(2,128)}, u32[]{:S(2)}) copy-start(f32[2,64]{1,0:T(2,128)} %head_gains.1) | copy-start | bytes 1540

commit v5 on v4

--- a/solution.py
+++ b/solution.py
@@ -42,18 +42,24 @@
 def body(
     lon_n,
     lat_n,
-    fine,
+    fine_hbm,
     coarse_in,
     norm_gains,
     kernels,
     token_gain,
     head_gains,
+    wq_hbm,
+    wkv_hbm,
+    wo_hbm,
+    we_hbm,
+    out_hbm,
+    coarse_out,
+    outs,
+    fine,
     wq,
     wkv,
     wo,
     we,
-    outs,
-    coarse_out,
     hb,
     x1,
     x2,
@@ -66,7 +72,9 @@
     cols_r,
     cols2_s,
     cols2_r,
+    dma,
     wsem,
+    osem,
     hs,
     hr,
     c2s,
@@ -109,7 +117,13 @@
                         wsem.at[len(taps)],
                     )
                 )
-    for copy in taps:
+    local = [
+        pltpu.make_async_copy(src, dst, dma.at[i])
+        for i, (src, dst) in enumerate(
+            ((fine_hbm, fine), (wq_hbm, wq), (wkv_hbm, wkv), (wo_hbm, wo), (we_hbm, we))
+        )
+    ]
+    for copy in local[:1] + taps + local[1:]:
         copy.start()
 
     cols_r[...] = jnp.zeros_like(cols_r)
@@ -185,11 +199,12 @@
             device_id_type=MESH,
         )
 
-    to_down = remote(fine.at[pl.ds(pairs - 1, 1)], halo.at[pl.ds(0, 1)], 0, (down, lat))
-    to_up = remote(fine.at[pl.ds(0, 1)], halo.at[pl.ds(1, 1)], 1, (up, lat))
+    to_down = remote(fine_hbm.at[pl.ds(pairs - 1, 1)], halo.at[pl.ds(0, 1)], 0, (down, lat))
+    to_up = remote(fine_hbm.at[pl.ds(0, 1)], halo.at[pl.ds(1, 1)], 1, (up, lat))
     to_down.start()
     to_up.start()
 
+    local[0].wait()
     cols_s[0] = fine[:, :, 0:16, :].astype(F32)[:, :, 0:1, :]
     cols_s[1] = fine[:, :, width - 16 : width, :].astype(F32)[:, :, 15:16, :]
     side_copies = []
@@ -328,6 +343,8 @@
     pl.when(has_west)(to_west.start)
     pl.when(has_east)(to_east.start)
 
+    for copy in local[1:]:
+        copy.wait()
     heads = wide // head_gains.shape[1]
     hd = wide // heads
     tg = token_gain[...]
@@ -391,6 +408,12 @@
     patch(x2, cols2_r)
     n2 = pairs // lon_t
 
+    def out_copy(i):
+        at = pl.multiple_of(i * n2, n2)
+        return pltpu.make_async_copy(
+            outs.at[pl.ds(at, n2)], out_hbm.at[pl.ds(at, n2)], osem.at[i]
+        )
+
     def third(i, c):
         results = [conv(x2, pl.multiple_of((2 * i + k) * n2, n2), n2, 1) for k in range(2)]
         for k in range(2):
@@ -402,9 +425,12 @@
                 outs[pl.ds(at, n2), q] = (
                     fine[pl.ds(at, n2), q].astype(F32) + v + up_row[None]
                 ).astype(BF16)
+            out_copy(2 * i + k).start()
         return c
 
     lax.fori_loop(0, lon_t // 2, third, 0)
+    for i in range(lon_t):
+        out_copy(i).wait()
 
 
 def local(lon_n, lat_n, fine_state, coarse_state, norm_gains, kernels, token_gain, head_gains,
@@ -415,6 +441,7 @@
     hops = lat_n // 2 + lon_n // 2
     tokens = own * lon_n * lat_n
     vm = pl.BlockSpec(memory_space=pltpu.VMEM)
+    hbm = pl.BlockSpec(memory_space=pltpu.HBM)
     sem = pltpu.SemaphoreType.DMA
     fine_result, coarse_result = pl.pallas_call(
         functools.partial(body, lon_n, lat_n),
@@ -422,9 +449,15 @@
             jax.ShapeDtypeStruct((pairs, 2, width, ch), BF16),
             jax.ShapeDtypeStruct(coarse_state.shape, BF16),
         ),
-        in_specs=[vm] * 10,
-        out_specs=(vm, vm),
+        in_specs=[hbm, vm, vm, hbm, vm, vm, hbm, hbm, hbm, hbm],
+        out_specs=(hbm, vm),
         scratch_shapes=[
+            pltpu.VMEM((pairs, 2, width, ch), BF16),
+            pltpu.VMEM((pairs, 2, width, ch), BF16),
+            pltpu.VMEM(query_weight.shape, BF16),
+            pltpu.VMEM(keyvalue_weight.shape, BF16),
+            pltpu.VMEM(output_weight.shape, BF16),
+            pltpu.VMEM(expand_weight.shape, BF16),
             pltpu.VMEM((2, 7, 2, width + 16, ch), F32),
             pltpu.VMEM((pairs + 2, width, 6 * ch), BF16),
             pltpu.VMEM((pairs + 1, width, 6 * ch), BF16),
@@ -437,7 +470,9 @@
             pltpu.VMEM((2, pairs + 2, 2, 1, ch), F32),
             pltpu.VMEM((2, pairs + 1, 2, 1, ch), F32),
             pltpu.VMEM((2, pairs + 1, 2, 1, ch), F32),
+            sem((5,)),
             sem((12,)),
+            sem((lon_t,)),
             sem((8,)),
             sem((8,)),
             sem((2,)),
@@ -446,7 +481,7 @@
             sem((2, hops)),
         ],
         compiler_params=pltpu.CompilerParams(
-            collective_id=0, has_side_effects=True, vmem_limit_bytes=36 * 2**20 + 2 * tokens * wide
+            collective_id=0, has_side_effects=True, vmem_limit_bytes=56 * 2**20
         ),
     )(
         fine_state.reshape(pairs, 2, width, ch),

time: 43.7 us -> 37.7 us (0.86)
  the two profiles are of different devices: /device:TPU:3 before, /device:TPU:0 now
where the time goes in v5:
time: 37.7 us; the launch traced here: 37 us
  Pallas kernels  32.7 us (87%)
  local copies, waits for them, and re-layouts  3.7 us (10%)
  between operations  0.65 us (2%)
    pallas_call x1, Pallas kernels, local(): pl.pallas_call(functools.partial(body, lon_n, lat_n), out_shape=(jax.Shap...  32.7 us
    unnamed x4, local copies, waits for them, and re-layouts  3.7 us

profile of v5, /device:TPU:0, one launch (start us, length us, event | category | flops | bytes accessed | tf_op | source)
XLA Modules:
  0.0 37.0 jit_solution(3901075517928727462)
XLA Ops:
  0.6 32.7 %shard_map.113 = (bf16[64,2,64,128]{3,2,1,0:T(8,128)(2,1)}, bf16[8,4,512]{2,1,0:T(4,128)(2,1)}) custom-call(bf16[64,2,64,128]{3,2,1,0:T(8,128)(2,1)} %bitcast.3, bf16[8,4,512]{2,1,0:T(4,128)(2,1)} %coarse_in.1, f32[2,128]{1,0:T(2,128)} %norm_gains.1, bf16[2,3,3,128,128]{4,3,2,1,0:T(8,128)(2,1)} %kernels.1, f32[1,512]{1,0:T(1,128)} %bitcast.5, ...), custom_call_target="tpu_custom_call" | custom-call | tf_op jit(solution)/shard_map/pallas_call | solution.py:446
  33.3 0.0 copy-start
  33.3 3.1 %copy.14 = bf16[128,64,128]{2,1,0:T(8,128)(2,1)} copy(bf16[128,64,128]{2,1,0:T(8,128)(2,1)} %bitcast.4) | data formatting | bytes 4194304
  36.4 0.0 copy-done
  36.4 0.6 %copy.15 = bf16[8,4,512]{2,1,0:T(4,128)(2,1)} copy(bf16[8,4,512]{2,1,0:T(4,128)(2,1)S(1)} %copy-done) | data formatting | bytes 65536
Async XLA Ops:
  33.3 3.1 %copy-start = (bf16[8,4,512]{2,1,0:T(4,128)(2,1)S(1)}, bf16[8,4,512]{2,1,0:T(4,128)(2,1)}, u32[]{:S(2)}) copy-start(bf16[8,4,512]{2,1,0:T(4,128)(2,1)} %get-tuple-element.9) | copy-start | bytes 98308

commit v6 on v5

--- a/solution.py
+++ b/solution.py
@@ -365,9 +365,9 @@
     head_mask = r == c
     qb = jnp.where(head_mask, jnp.concatenate([q] * heads, axis=0), 0.0).astype(BF16)
 
-    def attend(half, nt, i, carry):
+    def attend(nt, i, carry):
         acc, tot = carry
-        t = tok[half, pl.ds(pl.multiple_of(i * nt, nt), nt)].astype(F32)
+        t = tok[:, pl.ds(pl.multiple_of(i * nt, nt), nt)].reshape(2 * nt, wide).astype(F32)
         kv = mm(norm_tokens(t), wkv[...])
         k = norm_heads(kv[:, :wide], gk).astype(BF16)
         vv = kv[:, wide:].astype(BF16)
@@ -376,16 +376,14 @@
         return acc + mm(e.astype(BF16), vv), tot + jnp.sum(e, axis=1, keepdims=True)
 
     carry = (jnp.zeros((heads * own, wide), F32), jnp.zeros((heads * own, 1), F32))
-    done = [0, 0]
+    done = 0
     while True:
-        for half, ready in enumerate(held(state["at"])):
-            more = ready - done[half]
-            if more >= 128:
-                nt = 256 if more % 256 == 0 and done[half] % 256 == 0 else 128
-                carry = lax.fori_loop(
-                    done[half] // nt, ready // nt, functools.partial(attend, half, nt), carry
-                )
-                done[half] = ready
+        ready = min(held(state["at"]))
+        if ready - done >= 128:
+            nt = math.gcd(ready - done, 256)
+            nt = math.gcd(nt, done) if done else nt
+            carry = lax.fori_loop(done // nt, ready // nt, functools.partial(attend, nt), carry)
+            done = ready
         if state["at"] == 4:
             break
         advance()
@@ -431,6 +429,19 @@
     lax.fori_loop(0, lon_t // 2, third, 0)
     for i in range(lon_t):
         out_copy(i).wait()
+
+
+def hand_on(fine_in, coarse_in, fine_out, coarse_out, sems):
+    parts = sems.shape[0] - 1
+    n = fine_in.shape[0] // parts
+    copies = [pltpu.make_async_copy(coarse_in, coarse_out, sems.at[parts])]
+    for i in range(parts):
+        part = pl.ds(i * n, n)
+        copies.append(pltpu.make_async_copy(fine_in.at[part], fine_out.at[part], sems.at[i]))
+    for copy in copies:
+        copy.start()
+    for copy in copies:
+        copy.wait()
 
 
 def local(lon_n, lat_n, fine_state, coarse_state, norm_gains, kernels, token_gain, head_gains,
@@ -495,6 +506,18 @@
         output_weight,
         expand_weight,
     )
+    anywhere = pl.BlockSpec(memory_space=pl.ANY)
+    fine_result, coarse_result = pl.pallas_call(
+        hand_on,
+        out_shape=(
+            jax.ShapeDtypeStruct(fine_result.shape, BF16),
+            jax.ShapeDtypeStruct(coarse_result.shape, BF16),
+        ),
+        in_specs=[anywhere] * 2,
+        out_specs=(anywhere,) * 2,
+        scratch_shapes=[sem((lon_t + 1,))],
+        compiler_params=pltpu.CompilerParams(vmem_limit_bytes=60 * 2**20),
+    )(fine_result, coarse_result)
     return fine_result.reshape(fine_state.shape), coarse_result
 
 

time: 37.7 us -> 99.2 us (2.63)
  Pallas kernels: 32.7 us -> 97.9 us
  local copies, waits for them, and re-layouts: 3.7 us -> 0 us
    pallas_call x0 -> x1, Pallas kernels: none -> 65.7 us  [local(): pl.pallas_call(hand_on, out_shape=(jax.ShapeDtypeStruct(fine_result.shape...]
    unnamed x4 -> x0, local copies, waits for them, and re-layouts: 3.7 us -> none
where the time goes in v6:
time: 99.2 us; the launch traced here: 98.5 us
  Pallas kernels  97.9 us (99%)
    pallas_call x1, Pallas kernels, local(): pl.pallas_call(hand_on, out_shape=(jax.ShapeDtypeStruct(fine_result.shape...  65.7 us
    pallas_call x1, Pallas kernels, local(): pl.pallas_call(functools.partial(body, lon_n, lat_n), out_shape=(jax.Shap...  32.2 us

profile of v6, /device:TPU:0, one launch (start us, length us, event | category | flops | bytes accessed | tf_op | source)
XLA Modules:
  0.0 98.5 jit_solution(432377903627835744)
XLA Ops:
  0.6 32.2 %shard_map.113 = (bf16[64,2,64,128]{3,2,1,0:T(8,128)(2,1)}, bf16[8,4,512]{2,1,0:T(4,128)(2,1)}) custom-call(bf16[64,2,64,128]{3,2,1,0:T(8,128)(2,1)} %bitcast.3, bf16[8,4,512]{2,1,0:T(4,128)(2,1)} %coarse_in.1, f32[2,128]{1,0:T(2,128)} %norm_gains.1, bf16[2,3,3,128,128]{4,3,2,1,0:T(8,128)(2,1)} %kernels.1, f32[1,512]{1,0:T(1,128)} %bitcast.4, ...), custom_call_target="tpu_custom_call" | custom-call | tf_op jit(solution)/shard_map/pallas_call | solution.py:457
  32.8 65.7 %shard_map.114 = (bf16[64,2,64,128]{3,2,1,0:T(8,128)(2,1)}, bf16[8,4,512]{2,1,0:T(4,128)(2,1)}) custom-call(bf16[64,2,64,128]{3,2,1,0:T(8,128)(2,1)} %get-tuple-element.6.fine_in, bf16[8,4,512]{2,1,0:T(4,128)(2,1)} %get-tuple-element.7.coarse_in), custom_call_target="tpu_custom_call" | custom-call | tf_op jit(solution)/shard_map/pallas_call | solution.py:510

commit v7 on v6

--- a/solution.py
+++ b/solution.py
@@ -431,16 +431,21 @@
         out_copy(i).wait()
 
 
-def hand_on(fine_in, coarse_in, fine_out, coarse_out, sems):
-    parts = sems.shape[0] - 1
-    n = fine_in.shape[0] // parts
-    copies = [pltpu.make_async_copy(coarse_in, coarse_out, sems.at[parts])]
+def hand_on(fine_in, coarse_in, fine_out, coarse_out, fine, coarse, sems):
+    parts = sems.shape[1] - 1
+    n = fine.shape[0] // parts
+    moves = [(coarse_in, coarse, coarse_out)]
     for i in range(parts):
         part = pl.ds(i * n, n)
-        copies.append(pltpu.make_async_copy(fine_in.at[part], fine_out.at[part], sems.at[i]))
-    for copy in copies:
+        moves.append((fine_in.at[part], fine.at[part], fine_out.at[part]))
+    ins = [pltpu.make_async_copy(a, b, sems.at[0, i]) for i, (a, b, c) in enumerate(moves)]
+    outs = [pltpu.make_async_copy(b, c, sems.at[1, i]) for i, (a, b, c) in enumerate(moves)]
+    for copy in ins:
         copy.start()
-    for copy in copies:
+    for arrived, leaving in zip(ins, outs):
+        arrived.wait()
+        leaving.start()
+    for copy in outs:
         copy.wait()
 
 
@@ -515,7 +520,11 @@
         ),
         in_specs=[anywhere] * 2,
         out_specs=(anywhere,) * 2,
-        scratch_shapes=[sem((lon_t + 1,))],
+        scratch_shapes=[
+            pltpu.VMEM(fine_result.shape, BF16),
+            pltpu.VMEM(coarse_result.shape, BF16),
+            sem((2, lon_t + 1)),
+        ],
         compiler_params=pltpu.CompilerParams(vmem_limit_bytes=60 * 2**20),
     )(fine_result, coarse_result)
     return fine_result.reshape(fine_state.shape), coarse_result

time: 99.2 us -> 36 us (0.36)
  Pallas kernels: 97.9 us -> 34.6 us
    pallas_call x1, Pallas kernels: 65.7 us -> 2.43 us  [local(): pl.pallas_call(hand_on, out_shape=(jax.ShapeDtypeStruct(fine_result.shape...]
where the time goes in v7:
time: 36 us; the launch traced here: 35.2 us
  Pallas kernels  34.6 us (96%)
  between operations  0.64 us (2%)
    pallas_call x1, Pallas kernels, local(): pl.pallas_call(functools.partial(body, lon_n, lat_n), out_shape=(jax.Shap...  32.2 us
    pallas_call x1, Pallas kernels, local(): pl.pallas_call(hand_on, out_shape=(jax.ShapeDtypeStruct(fine_result.shape...  2.43 us

profile of v7, /device:TPU:0, one launch (start us, length us, event | category | flops | bytes accessed | tf_op | source)
XLA Modules:
  0.0 35.2 jit_solution(15431235915335056373)
XLA Ops:
  0.6 32.2 %shard_map.113 = (bf16[64,2,64,128]{3,2,1,0:T(8,128)(2,1)}, bf16[8,4,512]{2,1,0:T(4,128)(2,1)}) custom-call(bf16[64,2,64,128]{3,2,1,0:T(8,128)(2,1)} %bitcast.3, bf16[8,4,512]{2,1,0:T(4,128)(2,1)} %coarse_in.1, f32[2,128]{1,0:T(2,128)} %norm_gains.1, bf16[2,3,3,128,128]{4,3,2,1,0:T(8,128)(2,1)} %kernels.1, f32[1,512]{1,0:T(1,128)} %bitcast.4, ...), custom_call_target="tpu_custom_call" | custom-call | tf_op jit(solution)/shard_map/pallas_call | solution.py:462
  32.8 2.4 %shard_map.114 = (bf16[64,2,64,128]{3,2,1,0:T(8,128)(2,1)}, bf16[8,4,512]{2,1,0:T(4,128)(2,1)}) custom-call(bf16[64,2,64,128]{3,2,1,0:T(8,128)(2,1)} %get-tuple-element.6.fine_in, bf16[8,4,512]{2,1,0:T(4,128)(2,1)} %get-tuple-element.7.coarse_in), custom_call_target="tpu_custom_call" | custom-call | tf_op jit(solution)/shard_map/pallas_call | solution.py:515
